TPU v7x, 32 devices: a whole 2x2x4 slice. The times are simulated.
32 devices in a mesh: groups: 2 (over y), ep: 8 (over z, core), pd: 2 (over x).
Axes of the slice: x: 2, y: 2, z: 4, core: 2. Of those that a mesh axis runs over, the one named last changes fastest.
Arguments:
- hidden: bfloat16 [2048, 7168], P(('groups', 'ep', 'pd')), parts along dimension 0, may hold values from -6 to 6
- moe_gain: float32 [7168], replicated, may hold values from 0.4 to 1.6
- expert_ids: int32 [2048, 2], P(('groups', 'ep', 'pd')), parts along dimension 0, may hold values from 0 to 7, all different within a row; in each aligned block of 64 rows (0 to 63, 64 to 127, ...) at most 32 rows name the same one
- gate_scores: float32 [2048, 2], P(('groups', 'ep', 'pd')), parts along dimension 0, may hold values from 0.05 to 1
- gate_up: bfloat16 [8, 7168, 2, 1024], P('ep', None, None, 'pd'), may hold values from -0.0625 to 0.0625
- down_proj: bfloat16 [8, 1024, 7168], P('ep', 'pd'), may hold values from -0.1875 to 0.1875
- kv_weight: bfloat16 [7168, 576], P('ep'), may hold values from -0.0625 to 0.0625
- attn_gain: float32 [7168], replicated, may hold values from 0.4 to 1.6
- kv_gain: float32 [512], replicated, may hold values from 0.25 to 1.75
- prompt_lens: int32 [32], P('groups'), parts along dimension 0, may hold values from 1 to 192, 1024 in all
- assign: int32 [32], P('groups'), parts along dimension 0, may hold values from 0 to 15, each once
- latent_cache: bfloat16 [32, 512, 576], P(('groups', 'ep', 'pd')), parts along dimension 0, may hold values from -17 to 17
- cache_len: int32 [32], P(('groups', 'ep', 'pd')), parts along dimension 0, may hold values from 1 to 512, 4096 in all
- draft_hidden: bfloat16 [32, 4, 7168], P(('groups', 'ep', 'pd')), parts along dimension 0, may hold values from -6 to 6
- queries: bfloat16 [32, 4, 64, 576], P(('groups', 'ep', 'pd')), parts along dimension 0, may hold values from -140 to 140
Outputs:
- layer_out: bfloat16 [2048, 7168], P(('groups', 'ep', 'pd')), parts along dimension 0
- decoded: bfloat16 [32, 4, 64, 512], P(('groups', 'ep', 'pd')), parts along dimension 0
There are 2 independent parts, one for each index of `groups`. A program takes and returns all parts, laid end to end along the dimension named above; an argument that names none is the same for every part. Nothing has to cross between parts.
Inputs may be any that keep to these rules, and one draw needn't show every extreme that they name: `expert_ids`: each row names 2 different experts. Among the rows of one device (64 tokens) no expert is named more than 32 times, a bound that some block reaches. `prompt_lens`: the blocks lie end to end over all 1024 token rows, in order; the longest has 192 rows. `assign`: every slot receives exactly one prompt block. `cache_len`: some slot is full.
All inputs are finite; a program needn't handle non-finite values. No bound on the sum of `cache_len` on one device may be relied on, other than what follows from the above.
Results may differ from a plain program's by a relative error of at most 0.0086.
Values may be sent and summed in bfloat16 or wider, within the bound.
A program may use at most 128 MiB of HBM per device.

v0:
```python
import jax
import jax.numpy as jnp
from jax import lax
from jax.sharding import PartitionSpec as P

NORM_EPSILON = 1e-06
ROUTE_SCALE = 2.5
SCORE_SCALE = 192.0 ** (-0.5)
ROPE_BASE = 10000.0


def rms_norm(values, gain):
    return (
        values * lax.rsqrt(jnp.mean(values * values, axis=-1, keepdims=True) + NORM_EPSILON) * gain
    )


def with_rope(row_vals, positions, rotary_width):
    latent_width = row_vals.shape[-1] - rotary_width
    rotary = row_vals[..., latent_width:].astype(jnp.float32)
    frequency = ROPE_BASE ** (
        -jnp.arange(rotary_width // 2, dtype=jnp.float32) * 2.0 / rotary_width
    )
    angles = positions.astype(jnp.float32)[..., None] * frequency
    even_part = rotary[..., 0::2]
    odd_part = rotary[..., 1::2]
    turned = jnp.stack(
        [
            even_part * jnp.cos(angles) - odd_part * jnp.sin(angles),
            even_part * jnp.sin(angles) + odd_part * jnp.cos(angles),
        ],
        axis=-1,
    ).reshape(rotary.shape)
    return jnp.concatenate([row_vals[..., :latent_width], turned.astype(jnp.bfloat16)], axis=-1)


def slot_attention(query, cache_rows, block_rows, draft_rows, cached, block_len, latent_width):
    step_count, head_count, row_width = query.shape
    rotary_width = row_width - latent_width
    block_cap = block_rows.shape[0]
    cache_cap = cache_rows.shape[0]
    block_pos = cached + jnp.arange(block_cap, dtype=jnp.int32)
    draft_pos = cached + block_len + jnp.arange(step_count, dtype=jnp.int32)
    key_rows = jnp.concatenate(
        [
            cache_rows,
            with_rope(block_rows, block_pos, rotary_width),
            with_rope(draft_rows, draft_pos, rotary_width),
        ],
        axis=0,
    )
    head_pos = jnp.broadcast_to(draft_pos[:, None], (step_count, head_count))
    turned_query = with_rope(query, head_pos, rotary_width).reshape(
        step_count * head_count, row_width
    )
    live_cache = jnp.broadcast_to(
        (jnp.arange(cache_cap, dtype=jnp.int32) < cached)[None, :], (step_count, cache_cap)
    )
    live_block = jnp.broadcast_to(
        (jnp.arange(block_cap, dtype=jnp.int32) < block_len)[None, :], (step_count, block_cap)
    )
    step_ids = jnp.arange(step_count, dtype=jnp.int32)
    live_draft = step_ids[None, :] <= step_ids[:, None]
    live_rows = jnp.concatenate([live_cache, live_block, live_draft], axis=1)
    scores = (
        jnp.einsum("qk,nk->qn", turned_query, key_rows, preferred_element_type=jnp.float32)
        * SCORE_SCALE
    )
    scores = scores.reshape(step_count, head_count, -1)
    scores = jnp.where(live_rows[:, None, :], scores, -1e30)
    peak = jnp.max(scores, axis=-1, keepdims=True)
    expo = jnp.exp(scores - peak)
    weights = (expo / jnp.sum(expo, axis=-1, keepdims=True)).astype(jnp.bfloat16)
    output = jnp.dot(
        weights.reshape(step_count * head_count, -1),
        key_rows[:, :latent_width],
        preferred_element_type=jnp.float32,
    )
    return output.reshape(step_count, head_count, latent_width).astype(jnp.bfloat16)


def per_device(
    hidden,
    moe_gain,
    expert_ids,
    gate_scores,
    gate_up,
    down_proj,
    kv_weight,
    attn_gain,
    kv_gain,
    prompt_lens,
    assign,
    latent_cache,
    cache_len,
    draft_hidden,
    queries,
):
    tok_rows, model_width = hidden.shape
    top_count = expert_ids.shape[1]
    experts = lax.axis_size("ep")
    quarters = lax.axis_size("pd")
    capacity = max(2, 2 * tok_rows * top_count // experts)
    normed = rms_norm(hidden.astype(jnp.float32), moe_gain).astype(jnp.bfloat16)
    route_weight = ROUTE_SCALE * gate_scores / jnp.sum(gate_scores, axis=-1, keepdims=True)
    flat_ids = expert_ids.reshape(-1)
    one_hot = (flat_ids[:, None] == jnp.arange(experts, dtype=jnp.int32)[None, :]).astype(jnp.int32)
    slot_rank = jnp.sum(
        one_hot * (jnp.cumsum(one_hot, axis=0, dtype=jnp.int32) - 1), axis=1, dtype=jnp.int32
    )
    target = flat_ids * capacity + slot_rank
    select = (jnp.arange(experts * capacity, dtype=jnp.int32)[:, None] == target[None, :]).astype(
        jnp.bfloat16
    )
    repeated = jnp.repeat(normed, top_count, axis=0)
    outgoing = (
        jnp.dot(select, repeated, preferred_element_type=jnp.float32)
        .astype(jnp.bfloat16)
        .reshape(experts, capacity, model_width)
    )
    gate_local = gate_up[0]
    down_local = down_proj[0]
    copies = jnp.broadcast_to(
        outgoing[:, None], (experts, quarters, capacity, model_width)
    ).reshape(experts * quarters, capacity, model_width)
    arrived = lax.all_to_all(copies, ("ep", "pd"), split_axis=0, concat_axis=0, tiled=True)
    row_block = arrived.reshape(-1, model_width)
    gate_val = jnp.einsum("rd,dgf->rgf", row_block, gate_local, preferred_element_type=jnp.float32)
    partial_value = jnp.dot(
        (jax.nn.silu(gate_val[:, 0]) * gate_val[:, 1]).astype(jnp.bfloat16),
        down_local,
        preferred_element_type=jnp.float32,
    ).astype(jnp.bfloat16)
    partial_out = partial_value.reshape(arrived.shape)
    returned = lax.all_to_all(partial_out, ("ep", "pd"), split_axis=0, concat_axis=0, tiled=True)
    expert_out = jnp.sum(
        returned.reshape(experts, quarters, capacity, model_width), axis=1, dtype=jnp.float32
    ).astype(jnp.bfloat16)
    restored = jnp.dot(
        select.T, expert_out.reshape(-1, model_width), preferred_element_type=jnp.float32
    ).reshape(tok_rows, top_count, model_width)
    mixture = jnp.sum(restored * route_weight[:, :, None], axis=1)
    layer_out = (hidden.astype(jnp.float32) + mixture).astype(jnp.bfloat16)
    slot_count, step_count = (draft_hidden.shape[0], draft_hidden.shape[1])
    latent_width = kv_gain.shape[0]
    row_width = kv_weight.shape[1]
    kv_input = rms_norm(
        jnp.concatenate([layer_out, draft_hidden.reshape(-1, model_width)], axis=0).astype(
            jnp.float32
        ),
        attn_gain,
    ).astype(jnp.bfloat16)
    compressed = jnp.dot(
        kv_input,
        lax.all_gather(kv_weight, "ep", axis=0, tiled=True),
        preferred_element_type=jnp.float32,
    )
    latent_all = jnp.concatenate(
        [rms_norm(compressed[:, :latent_width], kv_gain), compressed[:, latent_width:]], axis=-1
    ).astype(jnp.bfloat16)
    prompt_latent = latent_all[:tok_rows]
    draft_latent = latent_all[tok_rows:].reshape(slot_count, step_count, row_width)
    device = lax.axis_index(("ep", "pd"))
    slot_ids = device * slot_count + jnp.arange(slot_count, dtype=jnp.int32)
    owner_hit = assign[None, :] == slot_ids[:, None]
    ends = jnp.cumsum(prompt_lens, dtype=jnp.int32)
    starts = ends - prompt_lens
    first_row = jnp.sum(jnp.where(owner_hit, starts[None, :], 0), axis=1, dtype=jnp.int32)
    block_len = jnp.sum(jnp.where(owner_hit, prompt_lens[None, :], 0), axis=1, dtype=jnp.int32)
    block_cap = 3 * tok_rows
    block_ids = jnp.arange(block_cap, dtype=jnp.int32)
    wanted = first_row[:, None] + block_ids[None, :]
    live_rows = block_ids[None, :] < block_len[:, None]
    shard_rows = lax.all_gather(prompt_latent, ("ep", "pd"), axis=0, tiled=True)
    row_index = jnp.arange(shard_rows.shape[0], dtype=jnp.int32)
    picker = ((row_index[None, None, :] == wanted[:, :, None]) & live_rows[:, :, None]).astype(
        jnp.bfloat16
    )
    blocks = jnp.einsum(
        "srn,nk->srk", picker, shard_rows, preferred_element_type=jnp.float32
    ).astype(jnp.bfloat16)
    decoded = jnp.stack(
        [
            slot_attention(
                queries[0],
                latent_cache[0],
                blocks[0],
                draft_latent[0],
                cache_len[0],
                block_len[0],
                latent_width,
            )
        ],
        axis=0,
    )
    return (layer_out, decoded)


def solution(mesh):
    in_specs = (
        P(("groups", "ep", "pd"), None),
        P(),
        P(("groups", "ep", "pd"), None),
        P(("groups", "ep", "pd"), None),
        P("ep", None, None, "pd"),
        P("ep", "pd", None),
        P("ep", None),
        P(),
        P(),
        P("groups"),
        P("groups"),
        P(("groups", "ep", "pd"), None, None),
        P(("groups", "ep", "pd")),
        P(("groups", "ep", "pd"), None, None),
        P(("groups", "ep", "pd"), None, None, None),
    )
    out_specs = (P(("groups", "ep", "pd"), None), P(("groups", "ep", "pd"), None, None, None))
    return jax.shard_map(
        per_device, mesh=mesh, in_specs=in_specs, out_specs=out_specs, check_vma=False
    )
```

profile of v0, /device:TPU:0, one launch (start us, length us, event | category | flops | bytes accessed | tf_op | source)
XLA Modules:
  0.0 501.0 jit_solution(12359630882984380079)
XLA Ops:
  7.2 0.8 copy.51
  7.9 0.1 reshape.239
  8.1 0.1 fusion.62
  8.2 0.2 reduce_window_sum.18
  8.3 0.2 select_reduce_fusion
  8.5 1.5 fusion.6
  10.0 1.5 fusion.8
  11.5 0.9 broadcast_in_dim.25
  12.4 1.7 reshape.240
  14.1 2.6 convolution_convert_fusion.1
  16.7 0.9 broadcast_in_dim.27
  17.6 0.0 slice-start
  17.6 168.0 %all_to_all.10 = bf16[16,32,7168]{2,1,0:T(8,128)(2,1)S(1)} all-to-all(bf16[16,32,7168]{2,1,0:T(8,128)(2,1)S(1)} %bitcast.57), channel_id=1, replica_groups=mesh['groups'=2,'ep'=8,'pd'=2] {'ep','pd'}, dimensions={0} | all-to-all | bytes 14680064 | tf_op jit(solution)/shard_map/all_to_all | solution.py:126
  185.7 11.5 %fusion = f32[512,2,512]{2,0,1:T(8,128)S(1)} fusion(bf16[512,7168,1]{1,0,2:T(8,128)(2,1)S(1)} %bitcast.61, bf16[7168,2,512]{2,1,0:T(2,128)(2,1)} %bitcast.74), kind=kOutput, calls=%fused_computation | convolution fusion | flops 7516192768 | bytes 24117248 | tf_op jit(solution)/shard_map/rd,dgf->rgf/dot_general | solution.py:128
  197.1 6.1 %convolution_convert_fusion = bf16[512,7168]{1,0:T(8,128)(2,1)} fusion(bf16[1,512,7168]{2,1,0:T(8,128)(2,1)S(1)} %bitcast.76, f32[512,2,512]{2,0,1:T(8,128)S(1)} %fusion), kind=kOutput, calls=%fused_computation.2 | convolution fusion | flops 3763339264 | bytes 16777216 | tf_op jit(solution)/shard_map/dot_general | solution.py:129
  203.2 4.9 all-to-all-start.1
  208.1 0.0 all-gather.3.cloned.1.call-start
  208.2 0.7 all-gather.3.cloned.1.call-update
  208.9 0.2 all-gather.5.cloned.1.call-start
  209.1 1.1 slice.65
  210.3 1.2 slice.66
  211.5 0.1 iota_compare_fusion.2
  211.6 0.1 copy.57
  211.7 0.1 reduce.7
  212.6 195.1 %all-to-all-done.1 = bf16[16,32,7168]{2,1,0:T(8,128)(2,1)} async-done(((bf16[16,32,7168]{2,1,0:T(8,128)(2,1)}), bf16[16,32,7168]{2,1,0:T(8,128)(2,1)}, u32[]{:S(2)}, u32[]{:S(2)}) %all-to-all-start.1) | async-done | bytes 7340064 | tf_op jit(solution)/shard_map/all_to_all | solution.py:135
  407.7 5.1 %bitcast_reduce_fusion = bf16[8,32,7168]{2,1,0:T(8,128)(2,1)S(1)} fusion(bf16[16,32,7168]{2,1,0:T(8,128)(2,1)} %all-to-all-done.1), kind=kLoop, calls=%fused_computation.5 | loop fusion | flops 1835008 | bytes 11010048 | tf_op jit(solution)/shard_map/reduce_sum | solution.py:136
  412.8 0.9 fusion.10
  413.7 0.3 copy-done
  414.0 0.2 fusion.9
  414.2 0.6 copy-done.4
  414.8 0.3 fusion.3
  415.2 0.0 all-gather.3.cloned.1.call-done
  415.2 6.0 %fusion.81 = (bf16[68,576]{1,0:T(8,128)(2,1)S(1)}, f32[68,576]{1,0:T(8,128)S(1)}) fusion(bf16[7168,576]{0,1:T(8,128)(2,1)} %all-gather.3.cloned.1.call-done, f32[7168]{0:T(1024)S(1)} %copy-done.5, f32[68]{0:T(128)S(1)} %add_rsqrt_fusion.1, bf16[4,7168]{1,0:T(4,128)(2,1)S(1)} %bitcast.71, bf16[64,7168]{1,0:T(8,128)(2,1)S(1)} %fusion.9), kind=kOutput, calls=%fused_computation.132 | convolution fusion | flops 564963584 | bytes 9496336 | tf_op jit(solution)/shard_map/dot_general | solution.py:153
  421.2 0.1 multiply_reduce_fusion
  421.3 0.1 multiply_convert_fusion
  421.4 0.6 pad_maximum_fusion.5
  422.1 0.0 all-gather.5.cloned.1.call-update
  422.1 0.7 fusion.76
  423.4 0.2 fusion.60
  423.6 0.1 copy.54
  423.8 0.1 copy.55
  423.9 0.6 iota_compare_fusion.7
  424.6 0.1 pad_add_fusion
  424.6 0.1 broadcast_in_dim.31
  424.7 0.3 copy.62
  425.0 0.3 copy.56
  425.3 0.6 iota_add_fusion
  426.0 0.1 slice.76
  426.2 0.1 slice.77
  426.3 0.1 fusion.74
  426.4 0.1 copy.60
  426.5 0.1 copy.61
  426.6 61.1 %all-gather.5.cloned.1.call-done = bf16[1024,576]{1,0:T(8,128)(2,1)} async-done(((bf16[64,576]{1,0:T(8,128)(2,1)}), bf16[1024,576]{1,0:T(8,128)(2,1)}) %all-gather.5.cloned.1.call-update) | async-done | bytes 1179664 | tf_op jit(solution)/shard_map/all_gather | solution.py:174
  487.7 1.9 convolution_convert_fusion.3
  489.6 0.9 slice.72
  490.5 0.9 slice.73
  491.4 0.4 fusion.64
  491.9 0.1 copy.58
  492.0 0.1 copy.59
  492.1 0.5 fusion.82
  492.7 0.2 fusion.37
  492.8 0.1 divide_convert_fusion
  492.9 0.2 copy.63
  493.1 1.1 fusion.12
  (48 shorter events, 0.4 us)
Async XLA Ops:
  17.6 179.5 %slice-start = ((s8[7340032]{0:T(1024)(128)(4,1)}), s8[3145728]{0:T(1024)(128)(4,1)S(1)}, s32[]{:S(2)}) async-start(s8[7340032]{0:T(1024)(128)(4,1)} %bitcast.75), calls=%async_computation.4 | async-start | bytes 6291456
  185.7 11.5 %slice-start.1 = ((s8[7340032]{0:T(1024)(128)(4,1)}), s8[4194304]{0:T(1024)(128)(4,1)S(1)}, s32[]{:S(2)}) async-start(s8[7340032]{0:T(1024)(128)(4,1)} %bitcast.75), calls=%async_computation.5 | async-start | bytes 8388608
  203.2 5.9 %copy-start.3 = (bf16[1,4,64,576]{3,2,1,0:T(8,128)(2,1)S(1)}, bf16[1,4,64,576]{3,2,1,0:T(8,128)(2,1)}, u32[]{:S(2)}) copy-start(bf16[1,4,64,576]{3,2,1,0:T(8,128)(2,1)} %param.29) | copy-start | bytes 884740
  203.2 204.5 %all-to-all-start.1 = ((bf16[16,32,7168]{2,1,0:T(8,128)(2,1)}), bf16[16,32,7168]{2,1,0:T(8,128)(2,1)}, u32[]{:S(2)}, u32[]{:S(2)}) async-start(bf16[16,32,7168]{2,1,0:T(8,128)(2,1)} %bitcast.60), calls=%async_computation.1 | async-start | bytes 14680064 | tf_op jit(solution)/shard_map/all_to_all | solution.py:135
  208.1 3.5 copy-start.8
  208.1 4.4 copy-start.6
  208.1 207.0 %all-gather.3.cloned.1.call-start = ((), (), s32[]{:S(2)}) async-start(), calls=%async_computation.2 | async-start | bytes 9289728 | tf_op jit(solution)/shard_map/all_gather | solution.py:155
  208.9 278.9 %all-gather.5.cloned.1.call-start = ((), (), s32[]{:S(2)}) async-start(), calls=%async_computation.3 | async-start | bytes 1392640 | tf_op jit(solution)/shard_map/all_gather | solution.py:174
  412.8 1.2 copy-start
  414.0 0.8 copy-start.4
  414.0 1.2 copy-start.5
  414.2 7.0 %copy-start.1 = (bf16[64,7168]{1,0:T(8,128)(2,1)}, bf16[64,7168]{1,0:T(8,128)(2,1)S(1)}, u32[]{:S(2)}) copy-start(bf16[64,7168]{1,0:T(8,128)(2,1)S(1)} %fusion.9) | copy-start | bytes 2752516
  415.1 6.2 %copy-start.7 = (f32[512]{0:T(512)S(1)}, f32[512]{0:T(512)}, u32[]{:S(2)}) copy-start(f32[512]{0:T(512)} %param.23) | copy-start | bytes 6148
  415.2 6.9 %copy-start.9 = (s32[16]{0:T(128)S(1)}, s32[16]{0:T(128)}, u32[]{:S(2)}) copy-start(s32[16]{0:T(128)} %param.25) | copy-start | bytes 196
  421.2 3.8 copy-start.2
Sparse Core Ops, SparseCore 0:
  210.6 177.3 all-gather.2
  422.2 65.4 all-gather.4
where the time goes:
time: 502 us; the launch traced here: 501 us
  waiting for transfers between devices  257 us (51%)
  blocking collectives  168 us (33%)
  matrix products  30.4 us (6%)
  between operations  15.9 us (3%)
  other arithmetic  13.2 us (3%)
  local copies, waits for them, and re-layouts  11.4 us (2%)
  starting transfers between devices  5.13 us (1%)
    all_to_all x1, waiting for transfers between devices, per_device(): lax.all_to_all(partial_out, ('ep', 'pd'), split_axis=0, concat_axis=0, ti...  195 us
    all_to_all x1, blocking collectives, per_device(): lax.all_to_all(copies, ('ep', 'pd'), split_axis=0, concat_axis=0, tiled=T...  168 us
    all_gather x1, waiting for transfers between devices, per_device(): shard_rows = lax.all_gather(prompt_latent, ('ep', 'pd'), axis=0, tiled=True)  61.1 us
    dot_general x1, matrix products, per_device(): jnp.einsum('rd,dgf->rgf', row_block, gate_local, preferred_element_type=j...  11.5 us
  transfers between devices with their start and end apart: 3, of which 2 were waited for; matrix products, arithmetic and copies ran while one was open for 3% of the time, Pallas kernels for 0%

commit v1 on v0

--- a/solution.py
+++ b/solution.py
@@ -1,6 +1,10 @@
+import functools
+
 import jax
 import jax.numpy as jnp
 from jax import lax
+from jax.experimental import pallas as pl
+from jax.experimental.pallas import tpu as pltpu
 from jax.sharding import PartitionSpec as P
 
 NORM_EPSILON = 1e-06
@@ -77,6 +81,213 @@
         preferred_element_type=jnp.float32,
     )
     return output.reshape(step_count, head_count, latent_width).astype(jnp.bfloat16)
+
+
+def peer_order(count):
+    order = []
+    far, near = count // 2, 1
+    for distance in (far, near, count - 1):
+        if 0 < distance < count and distance not in order:
+            order.append(distance)
+    for distance in range(1, count):
+        if distance not in order:
+            order.append(distance)
+    return order
+
+
+def meet_peers(ep_size, pd_size):
+    me, column = lax.axis_index("ep"), lax.axis_index("pd")
+    barrier = pltpu.get_barrier_semaphore()
+    for distance in range(1, ep_size):
+        pl.semaphore_signal(
+            barrier,
+            inc=1,
+            device_id={"ep": lax.rem(me + distance, ep_size)},
+            device_id_type=pl.DeviceIdType.MESH,
+        )
+    for distance in range(1, pd_size):
+        pl.semaphore_signal(
+            barrier,
+            inc=1,
+            device_id={"pd": lax.rem(column + distance, pd_size)},
+            device_id_type=pl.DeviceIdType.MESH,
+        )
+    pl.semaphore_wait(barrier, ep_size - 1 + pd_size - 1)
+
+
+def spread_kernel(
+    ep_size, pd_size, shared, pieces, src, out, local_sem, send_sem, recv_sem, pass_sem, got_sem
+):
+    me, column = lax.axis_index("ep"), lax.axis_index("pd")
+    width = out.shape[-1] // pieces
+    order = peer_order(ep_size)
+    meet_peers(ep_size, pd_size)
+
+    def part(ref, piece):
+        return ref if pieces == 1 else ref.at[:, pl.ds(piece * width, width)]
+
+    def block(target):
+        return src if shared else src.at[target]
+
+    def direct(distance, piece):
+        target = lax.rem(me + distance, ep_size)
+        return pltpu.make_async_remote_copy(
+            src_ref=part(block(target), piece),
+            dst_ref=part(out.at[column, me], piece),
+            send_sem=send_sem.at[distance, piece],
+            recv_sem=recv_sem.at[distance, piece],
+            device_id={"ep": target},
+            device_id_type=pl.DeviceIdType.MESH,
+        )
+
+    def across(owner, from_src, step, distance, piece):
+        whole = block(me) if from_src else out.at[column, owner]
+        return pltpu.make_async_remote_copy(
+            src_ref=part(whole, piece),
+            dst_ref=part(out.at[column, owner], piece),
+            send_sem=pass_sem.at[step, distance, piece],
+            recv_sem=got_sem.at[step, distance, piece],
+            device_id={"pd": lax.rem(column + step, pd_size)},
+            device_id_type=pl.DeviceIdType.MESH,
+        )
+
+    own = pltpu.make_async_copy(block(me), out.at[column, me], local_sem)
+    own.start()
+    for piece in range(pieces):
+        for step in range(1, pd_size):
+            across(me, True, step, 0, piece).start()
+    for distance in order:
+        for piece in range(pieces):
+            direct(distance, piece).start()
+    for distance in order:
+        for piece in range(pieces):
+            owner = lax.rem(me - distance + ep_size, ep_size)
+            direct(distance, piece).wait_recv()
+            for step in range(1, pd_size):
+                across(owner, False, step, distance, piece).start()
+    own.wait()
+    for distance in order:
+        for piece in range(pieces):
+            direct(distance, piece).wait_send()
+    for distance in [0] + order:
+        for piece in range(pieces):
+            owner = lax.rem(me - distance + ep_size, ep_size)
+            for step in range(1, pd_size):
+                copy = across(owner, distance == 0, step, distance, piece)
+                copy.wait_send()
+                copy.wait_recv()
+
+
+def spread(source, block_shape, shared, pieces, collective_id, space):
+    ep_size, pd_size = lax.axis_size("ep"), lax.axis_size("pd")
+    return pl.pallas_call(
+        functools.partial(spread_kernel, ep_size, pd_size, shared, pieces),
+        out_shape=jax.ShapeDtypeStruct((pd_size, ep_size) + block_shape, source.dtype),
+        in_specs=[pl.BlockSpec(memory_space=space)],
+        out_specs=pl.BlockSpec(memory_space=space),
+        scratch_shapes=[
+            pltpu.SemaphoreType.DMA,
+            pltpu.SemaphoreType.DMA((ep_size, pieces)),
+            pltpu.SemaphoreType.DMA((ep_size, pieces)),
+            pltpu.SemaphoreType.DMA((pd_size, ep_size, pieces)),
+            pltpu.SemaphoreType.DMA((pd_size, ep_size, pieces)),
+        ],
+        compiler_params=pltpu.CompilerParams(
+            collective_id=collective_id, has_side_effects=True, vmem_limit_bytes=40 * 2**20
+        ),
+    )(source)
+
+
+def collect_kernel(
+    ep_size,
+    pd_size,
+    partial_out,
+    out,
+    own_rows,
+    other_rows,
+    summed,
+    own_sem,
+    local_sem,
+    pass_sem,
+    got_sem,
+    send_sem,
+    recv_sem,
+):
+    me, column = lax.axis_index("ep"), lax.axis_index("pd")
+    order = peer_order(ep_size) + [0]
+    meet_peers(ep_size, pd_size)
+
+    def across(distance, step):
+        target = lax.rem(me + distance, ep_size)
+        there = lax.rem(column + step, pd_size)
+        return pltpu.make_async_remote_copy(
+            src_ref=partial_out.at[there, target],
+            dst_ref=other_rows.at[step - 1, target],
+            send_sem=pass_sem.at[step, distance],
+            recv_sem=got_sem.at[step, distance],
+            device_id={"pd": there},
+            device_id_type=pl.DeviceIdType.MESH,
+        )
+
+    def direct(distance):
+        target = lax.rem(me + distance, ep_size)
+        return pltpu.make_async_remote_copy(
+            src_ref=summed.at[target],
+            dst_ref=out.at[me],
+            send_sem=send_sem.at[distance],
+            recv_sem=recv_sem.at[distance],
+            device_id={"ep": target},
+            device_id_type=pl.DeviceIdType.MESH,
+        )
+
+    fetch = pltpu.make_async_copy(partial_out.at[column], own_rows, own_sem)
+    fetch.start()
+    for distance in order:
+        for step in range(1, pd_size):
+            across(distance, step).start()
+    fetch.wait()
+    for distance in order:
+        target = lax.rem(me + distance, ep_size)
+        total = own_rows[target].astype(jnp.float32)
+        for step in range(1, pd_size):
+            across(distance, step).wait_recv()
+            total = total + other_rows[step - 1, target].astype(jnp.float32)
+        summed[target] = total.astype(jnp.bfloat16)
+        if distance:
+            direct(distance).start()
+    keep = pltpu.make_async_copy(summed.at[me], out.at[me], local_sem)
+    keep.start()
+    for distance in order:
+        for step in range(1, pd_size):
+            across(distance, step).wait_send()
+        if distance:
+            direct(distance).wait_send()
+            direct(distance).wait_recv()
+    keep.wait()
+
+
+def collect(partial_out, collective_id):
+    pd_size, ep_size, capacity, width = partial_out.shape
+    return pl.pallas_call(
+        functools.partial(collect_kernel, ep_size, pd_size),
+        out_shape=jax.ShapeDtypeStruct((ep_size, capacity, width), jnp.bfloat16),
+        in_specs=[pl.BlockSpec(memory_space=pl.ANY)],
+        out_specs=pl.BlockSpec(memory_space=pl.ANY),
+        scratch_shapes=[
+            pltpu.VMEM((ep_size, capacity, width), jnp.bfloat16),
+            pltpu.VMEM((pd_size - 1, ep_size, capacity, width), jnp.bfloat16),
+            pltpu.VMEM((ep_size, capacity, width), jnp.bfloat16),
+            pltpu.SemaphoreType.DMA,
+            pltpu.SemaphoreType.DMA,
+            pltpu.SemaphoreType.DMA((pd_size, ep_size)),
+            pltpu.SemaphoreType.DMA((pd_size, ep_size)),
+            pltpu.SemaphoreType.DMA((ep_size,)),
+            pltpu.SemaphoreType.DMA((ep_size,)),
+        ],
+        compiler_params=pltpu.CompilerParams(
+            collective_id=collective_id, has_side_effects=True, vmem_limit_bytes=48 * 2**20
+        ),
+    )(partial_out)
 
 
 def per_device(
@@ -109,21 +320,19 @@
         one_hot * (jnp.cumsum(one_hot, axis=0, dtype=jnp.int32) - 1), axis=1, dtype=jnp.int32
     )
     target = flat_ids * capacity + slot_rank
-    select = (jnp.arange(experts * capacity, dtype=jnp.int32)[:, None] == target[None, :]).astype(
-        jnp.bfloat16
-    )
-    repeated = jnp.repeat(normed, top_count, axis=0)
+    hits = jnp.arange(experts * capacity, dtype=jnp.int32)[:, None, None] == target.reshape(
+        1, tok_rows, top_count
+    )
+    select = jnp.any(hits, axis=-1).astype(jnp.bfloat16)
+    mix = jnp.sum(jnp.where(hits, route_weight[None], 0.0), axis=-1)
     outgoing = (
-        jnp.dot(select, repeated, preferred_element_type=jnp.float32)
+        jnp.dot(select, normed, preferred_element_type=jnp.float32)
         .astype(jnp.bfloat16)
         .reshape(experts, capacity, model_width)
     )
     gate_local = gate_up[0]
     down_local = down_proj[0]
-    copies = jnp.broadcast_to(
-        outgoing[:, None], (experts, quarters, capacity, model_width)
-    ).reshape(experts * quarters, capacity, model_width)
-    arrived = lax.all_to_all(copies, ("ep", "pd"), split_axis=0, concat_axis=0, tiled=True)
+    arrived = spread(outgoing, (capacity, model_width), False, 2, 1, pl.ANY)
     row_block = arrived.reshape(-1, model_width)
     gate_val = jnp.einsum("rd,dgf->rgf", row_block, gate_local, preferred_element_type=jnp.float32)
     partial_value = jnp.dot(
@@ -132,14 +341,16 @@
         preferred_element_type=jnp.float32,
     ).astype(jnp.bfloat16)
     partial_out = partial_value.reshape(arrived.shape)
-    returned = lax.all_to_all(partial_out, ("ep", "pd"), split_axis=0, concat_axis=0, tiled=True)
-    expert_out = jnp.sum(
-        returned.reshape(experts, quarters, capacity, model_width), axis=1, dtype=jnp.float32
-    ).astype(jnp.bfloat16)
-    restored = jnp.dot(
-        select.T, expert_out.reshape(-1, model_width), preferred_element_type=jnp.float32
-    ).reshape(tok_rows, top_count, model_width)
-    mixture = jnp.sum(restored * route_weight[:, :, None], axis=1)
+    expert_out = collect(partial_out, 2).reshape(-1, model_width)
+    mix_high = mix.astype(jnp.bfloat16)
+    mix_low = (mix - mix_high.astype(jnp.float32)).astype(jnp.bfloat16)
+    both = jnp.einsum(
+        "asr,sd->ard",
+        jnp.stack([mix_high, mix_low]),
+        expert_out,
+        preferred_element_type=jnp.float32,
+    )
+    mixture = both[0] + both[1]
     layer_out = (hidden.astype(jnp.float32) + mixture).astype(jnp.bfloat16)
     slot_count, step_count = (draft_hidden.shape[0], draft_hidden.shape[1])
     latent_width = kv_gain.shape[0]
@@ -150,10 +361,16 @@
         ),
         attn_gain,
     ).astype(jnp.bfloat16)
-    compressed = jnp.dot(
-        kv_input,
-        lax.all_gather(kv_weight, "ep", axis=0, tiled=True),
-        preferred_element_type=jnp.float32,
+    all_rows = kv_input.shape[0]
+    slices = kv_input.reshape(all_rows, experts, -1).swapaxes(0, 1)
+    gathered = lax.all_to_all(slices, "ep", split_axis=0, concat_axis=0, tiled=True)
+    pieces = jnp.einsum(
+        "erk,kl->erl", gathered, kv_weight, preferred_element_type=jnp.float32
+    ).astype(jnp.bfloat16)
+    compressed = jnp.sum(
+        lax.all_to_all(pieces, "ep", split_axis=0, concat_axis=0, tiled=True),
+        axis=0,
+        dtype=jnp.float32,
     )
     latent_all = jnp.concatenate(
         [rms_norm(compressed[:, :latent_width], kv_gain), compressed[:, latent_width:]], axis=-1
@@ -171,8 +388,12 @@
     block_ids = jnp.arange(block_cap, dtype=jnp.int32)
     wanted = first_row[:, None] + block_ids[None, :]
     live_rows = block_ids[None, :] < block_len[:, None]
-    shard_rows = lax.all_gather(prompt_latent, ("ep", "pd"), axis=0, tiled=True)
-    row_index = jnp.arange(shard_rows.shape[0], dtype=jnp.int32)
+    shard_rows = spread(prompt_latent, prompt_latent.shape, True, 1, 3, pltpu.VMEM).reshape(
+        -1, row_width
+    )
+    places = jnp.arange(quarters * experts * tok_rows, dtype=jnp.int32)
+    from_pd, from_ep = places // (experts * tok_rows), places // tok_rows % experts
+    row_index = (from_ep * quarters + from_pd) * tok_rows + places % tok_rows
     picker = ((row_index[None, None, :] == wanted[:, :, None]) & live_rows[:, :, None]).astype(
         jnp.bfloat16
     )

time: 502 us -> 333 us (0.66)
  Pallas kernels: 0 us -> 236 us
  waiting for transfers between devices: 257 us -> 36.7 us
  blocking collectives: 168 us -> 0 us
  between operations: 15.9 us -> 2.54 us
  starting transfers between devices: 5.13 us -> 10.4 us
    pallas_call x0 -> x3, Pallas kernels: none -> 236 us  [the longest x2 147 us: spread(): pl.pallas_call(functools.partial(spread_kernel, ep_size, pd_size, shared,...]
    all_to_all x1 -> x0, blocking collectives: 168 us -> none  [per_device(): lax.all_to_all(copies, ('ep', 'pd'), split_axis=0, concat_axis=0, tiled=T...]
    all_to_all x1 -> x2, waiting for transfers between devices: 195 us -> 36.7 us  [the longest x1 23 us: per_device(): lax.all_to_all(slices, 'ep', split_axis=0, concat_axis=0, tiled=True)]
    all_gather x2 -> x0, waiting for transfers between devices: 61.1 us -> none  [the longest x1 61.1 us: per_device(): shard_rows = lax.all_gather(prompt_latent, ('ep', 'pd'), axis=0, tiled=True)]
    all_to_all x1 -> x2, starting transfers between devices: 4.87 us -> 10.4 us  [the longest x1 6.59 us: per_device(): lax.all_to_all(slices, 'ep', split_axis=0, concat_axis=0, tiled=True)]
  transfers between devices with their start and end apart: 3 -> 2, of which waited for: 2 -> 2; matrix products, arithmetic and copies ran while one was open for 3% -> 2% of each run, Pallas kernels for 0% -> 0%
where the time goes in v1:
time: 333 us
  Pallas kernels  236 us (71%)
  waiting for transfers between devices  36.7 us (11%)
  matrix products  26.8 us (8%)
  local copies, waits for them, and re-layouts  10.5 us (3%)
  starting transfers between devices  10.4 us (3%)
  other arithmetic  9.33 us (3%)
    pallas_call x2, Pallas kernels, spread(): pl.pallas_call(functools.partial(spread_kernel, ep_size, pd_size, shared,...  147 us
    pallas_call x1, Pallas kernels, collect(): pl.pallas_call(functools.partial(collect_kernel, ep_size, pd_size), out_s...  88.8 us
    all_to_all x1, waiting for transfers between devices, per_device(): lax.all_to_all(slices, 'ep', split_axis=0, concat_axis=0, tiled=True)  23 us
    all_to_all x1, waiting for transfers between devices, per_device(): lax.all_to_all(pieces, 'ep', split_axis=0, concat_axis=0, tiled=True)  13.7 us
    dot_general x1, matrix products, per_device(): jnp.einsum('rd,dgf->rgf', row_block, gate_local, preferred_element_type=j...  11.5 us
  transfers between devices with their start and end apart: 2, of which 2 were waited for; matrix products, arithmetic and copies ran while one was open for 2% of the time, Pallas kernels for 0%

profile of v1, /device:TPU:0, one launch (start us, length us, event | category | flops | bytes accessed | tf_op | source)
XLA Modules:
  0.0 332.5 jit_solution(4971813422888057309)
XLA Ops:
  0.6 0.9 copy.77
  1.5 0.1 eq.70
  1.6 0.1 fusion.66
  1.7 0.2 reduce_window_sum.18
  1.9 0.2 select_reduce_fusion.1
  2.1 0.1 reduce_sum.95
  2.2 0.1 copy.78
  2.3 0.7 multiply_add_fusion
  3.0 0.1 fusion.54
  3.1 1.5 fusion.3
  4.6 2.4 convolution_convert_fusion.1
  7.0 122.5 %shard_map.158 = bf16[2,8,32,7168]{3,2,1,0:T(8,128)(2,1)S(1)} custom-call(bf16[8,32,7168]{2,1,0:T(8,128)(2,1)S(1)} %bitcast.79), custom_call_target="tpu_custom_call" | custom-call | tf_op jit(solution)/shard_map/pallas_call | solution.py:183
  129.5 11.5 %fusion = f32[512,2,512]{2,0,1:T(8,128)S(1)} fusion(bf16[512,7168,1]{1,0,2:T(8,128)(2,1)S(1)} %bitcast.80, bf16[7168,2,512]{2,1,0:T(2,128)(2,1)} %bitcast.97), kind=kOutput, calls=%fused_computation | convolution fusion | flops 7516192768 | bytes 24117248 | tf_op jit(solution)/shard_map/rd,dgf->rgf/dot_general | solution.py:337
  141.0 6.1 %convolution_convert_fusion = bf16[512,7168]{1,0:T(8,128)(2,1)} fusion(bf16[1,512,7168]{2,1,0:T(8,128)(2,1)S(1)} %bitcast.99, f32[512,2,512]{2,0,1:T(8,128)S(1)} %fusion), kind=kOutput, calls=%fused_computation.2 | convolution fusion | flops 3763339264 | bytes 16777216 | tf_op jit(solution)/shard_map/dot_general | solution.py:338
  147.1 88.8 %shard_map.159 = bf16[8,32,7168]{2,1,0:T(8,128)(2,1)S(1)} custom-call(bf16[2,8,32,7168]{3,2,1,0:T(8,128)(2,1)} %bitcast.83), custom_call_target="tpu_custom_call" | custom-call | tf_op jit(solution)/shard_map/pallas_call | solution.py:271
  235.9 1.8 copy-done.1
  237.7 0.1 select_reduce_fusion
  237.9 2.8 fusion.61
  240.7 0.2 fusion.6
  240.9 0.1 copy.95
  241.1 0.4 copy-done.6
  241.4 0.1 copy-done.5
  241.5 0.3 multiply_reduce_fusion
  241.9 1.3 fusion.11
  243.2 6.6 %all-to-all-start = ((bf16[8,68,896]{2,1,0:T(8,128)(2,1)}), bf16[8,68,896]{2,1,0:T(8,128)(2,1)S(1)}, u32[]{:S(2)}, u32[]{:S(2)}) async-start(bf16[8,68,896]{2,1,0:T(8,128)(2,1)} %fusion.11), calls=%async_computation | async-start | bytes 2064384 | tf_op jit(solution)/shard_map/all_to_all | solution.py:366
  249.8 0.1 copy.83
  249.9 0.1 reduce.6
  250.7 0.7 fusion.94
  251.4 0.7 iota_compare_fusion.4
  252.1 0.9 slice_convert_fusion
  253.0 23.0 %all-to-all-done = bf16[8,68,896]{2,1,0:T(8,128)(2,1)S(1)} async-done(((bf16[8,68,896]{2,1,0:T(8,128)(2,1)}), bf16[8,68,896]{2,1,0:T(8,128)(2,1)S(1)}, u32[]{:S(2)}, u32[]{:S(2)}) %all-to-all-start) | async-done | bytes 974880 | tf_op jit(solution)/shard_map/all_to_all | solution.py:366
  276.0 2.0 convolution_convert_fusion.2
  278.0 3.9 %all-to-all-start.1 = ((bf16[8,68,576]{2,1,0:T(8,128)(2,1)}), bf16[8,68,576]{2,1,0:T(8,128)(2,1)S(1)}, u32[]{:S(2)}, u32[]{:S(2)}) async-start(bf16[8,68,576]{2,1,0:T(8,128)(2,1)} %convolution_convert_fusion.2), calls=%async_computation.1 | async-start | bytes 1474560 | tf_op jit(solution)/shard_map/all_to_all | solution.py:371
  281.9 0.1 pad_add_fusion
  281.9 1.2 slice.74
  283.1 1.1 slice.73
  284.2 1.0 slice.91
  285.3 0.3 copy.89
  286.3 0.2 fusion.60
  286.6 0.1 copy.80
  286.7 0.1 copy.81
  286.8 0.3 copy.82
  287.1 0.7 iota_add_fusion
  287.8 13.7 %all-to-all-done.1 = bf16[8,68,576]{2,1,0:T(8,128)(2,1)S(1)} async-done(((bf16[8,68,576]{2,1,0:T(8,128)(2,1)}), bf16[8,68,576]{2,1,0:T(8,128)(2,1)S(1)}, u32[]{:S(2)}, u32[]{:S(2)}) %all-to-all-start.1) | async-done | bytes 626720 | tf_op jit(solution)/shard_map/all_to_all | solution.py:371
  301.5 0.1 convert_reduce_fusion
  301.7 0.1 slice.85
  301.8 0.1 slice.84
  301.9 0.1 multiply_reduce_fusion.1
  302.1 0.1 multiply_convert_fusion.1
  302.2 24.9 %shard_map.160 = bf16[2,8,64,576]{3,2,1,0:T(8,128)(2,1)S(1)} custom-call(bf16[64,576]{1,0:T(8,128)(2,1)S(1)} %pad_maximum_fusion.3.src), custom_call_target="tpu_custom_call" | custom-call | tf_op jit(solution)/shard_map/pallas_call | solution.py:183
  327.1 0.5 convolution_convert_fusion.4
  327.6 0.9 slice.81
  328.5 0.9 slice.80
  329.4 0.1 fusion.92
  329.5 0.1 copy.87
  329.6 0.1 copy.88
  329.7 0.5 fusion.68
  330.2 0.1 copy.85
  330.4 0.1 copy.86
  330.5 0.5 fusion.99
  331.0 0.2 fusion.36
  331.2 0.1 divide_convert_fusion
  331.3 0.2 copy.90
  331.5 1.1 fusion.9
  (52 shorter events, 0.5 us)
Async XLA Ops:
  0.6 275.4 %copy-start = (bf16[896,576]{0,1:T(8,128)(2,1)S(1)}, bf16[896,576]{0,1:T(8,128)(2,1)}, u32[]{:S(2)}) copy-start(bf16[896,576]{0,1:T(8,128)(2,1)} %param.21) | copy-start | bytes 3096580
  7.0 134.0 %slice-start = ((s8[7340032]{0:T(1024)(128)(4,1)}), s8[3145728]{0:T(1024)(128)(4,1)S(1)}, s32[]{:S(2)}) async-start(s8[7340032]{0:T(1024)(128)(4,1)} %bitcast.98), calls=%async_computation.2 | async-start | bytes 6291456
  129.5 11.5 %slice-start.1 = ((s8[7340032]{0:T(1024)(128)(4,1)}), s8[4194304]{0:T(1024)(128)(4,1)S(1)}, s32[]{:S(2)}) async-start(s8[7340032]{0:T(1024)(128)(4,1)} %bitcast.98), calls=%async_computation.3 | async-start | bytes 8388608
  147.1 90.7 %copy-start.7 = (f32[64,2]{0,1:T(2,128)S(1)}, f32[64,2]{0,1:T(2,128)}, u32[]{:S(2)}) copy-start(f32[64,2]{0,1:T(2,128)} %param.18) | copy-start | bytes 1540
  235.9 1.8 copy-start.1
  237.9 2.8 copy-start.3
  240.7 0.8 copy-start.6
  240.7 0.8 copy-start.5
  240.9 2.2 copy-start.2
  241.8 7.9 %copy-start.9 = (s32[16]{0:T(128)S(1)}, s32[16]{0:T(128)}, u32[]{:S(2)}) copy-start(s32[16]{0:T(128)} %param.24) | copy-start | bytes 196
  241.8 8.8 %copy-start.10 = (s32[16]{0:T(128)S(1)}, s32[16]{0:T(128)}, u32[]{:S(2)}) copy-start(s32[16]{0:T(128)} %param.25) | copy-start | bytes 196
  243.2 32.8 %all-to-all-start = ((bf16[8,68,896]{2,1,0:T(8,128)(2,1)}), bf16[8,68,896]{2,1,0:T(8,128)(2,1)S(1)}, u32[]{:S(2)}, u32[]{:S(2)}) async-start(bf16[8,68,896]{2,1,0:T(8,128)(2,1)} %fusion.11), calls=%async_computation | async-start | bytes 2064384 | tf_op jit(solution)/shard_map/all_to_all | solution.py:366
  278.0 8.8 %copy-start.4 = (bf16[1,512,576]{1,2,0:T(8,128)(2,1)S(1)}, bf16[1,512,576]{1,2,0:T(8,128)(2,1)}, u32[]{:S(2)}) copy-start(bf16[1,512,576]{1,2,0:T(8,128)(2,1)} %param.26) | copy-start | bytes 1769476
  278.0 23.5 %all-to-all-start.1 = ((bf16[8,68,576]{2,1,0:T(8,128)(2,1)}), bf16[8,68,576]{2,1,0:T(8,128)(2,1)S(1)}, u32[]{:S(2)}, u32[]{:S(2)}) async-start(bf16[8,68,576]{2,1,0:T(8,128)(2,1)} %convolution_convert_fusion.2), calls=%async_computation.1 | async-start | bytes 1474560 | tf_op jit(solution)/shard_map/all_to_all | solution.py:371
  286.3 15.7 %copy-start.8 = (f32[512]{0:T(512)S(1)}, f32[512]{0:T(512)}, u32[]{:S(2)}) copy-start(f32[512]{0:T(512)} %param.23) | copy-start | bytes 6148

commit v2 on v1

--- a/solution.py
+++ b/solution.py
@@ -83,16 +83,15 @@
     return output.reshape(step_count, head_count, latent_width).astype(jnp.bfloat16)
 
 
-def peer_order(count):
-    order = []
-    far, near = count // 2, 1
-    for distance in (far, near, count - 1):
-        if 0 < distance < count and distance not in order:
-            order.append(distance)
-    for distance in range(1, count):
-        if distance not in order:
-            order.append(distance)
-    return order
+def near_and_far(count):
+    return list(range(1, count // 2)), list(range(max(1, count // 2), count))
+
+
+def interleave(far, near):
+    merged = []
+    for i in range(max(len(far), len(near))):
+        merged += near[i : i + 1] + far[i : i + 1]
+    return merged
 
 
 def meet_peers(ep_size, pd_size):
@@ -115,76 +114,83 @@
     pl.semaphore_wait(barrier, ep_size - 1 + pd_size - 1)
 
 
+def remote(src, dst, send_sem, recv_sem, device):
+    return pltpu.make_async_remote_copy(
+        src_ref=src,
+        dst_ref=dst,
+        send_sem=send_sem,
+        recv_sem=recv_sem,
+        device_id=device,
+        device_id_type=pl.DeviceIdType.MESH,
+    )
+
+
 def spread_kernel(
-    ep_size, pd_size, shared, pieces, src, out, local_sem, send_sem, recv_sem, pass_sem, got_sem
+    ep_size, pd_size, pieces, window, src, out, local_sem, send_sem, recv_sem, pass_sem, got_sem
 ):
     me, column = lax.axis_index("ep"), lax.axis_index("pd")
     width = out.shape[-1] // pieces
-    order = peer_order(ep_size)
+    near, far = near_and_far(ep_size)
+    near = [(mask, piece) for mask in near for piece in range(pieces)]
+    far = [(mask, piece) for mask in far for piece in range(pieces)]
     meet_peers(ep_size, pd_size)
 
     def part(ref, piece):
         return ref if pieces == 1 else ref.at[:, pl.ds(piece * width, width)]
 
-    def block(target):
-        return src if shared else src.at[target]
-
-    def direct(distance, piece):
-        target = lax.rem(me + distance, ep_size)
-        return pltpu.make_async_remote_copy(
-            src_ref=part(block(target), piece),
-            dst_ref=part(out.at[column, me], piece),
-            send_sem=send_sem.at[distance, piece],
-            recv_sem=recv_sem.at[distance, piece],
-            device_id={"ep": target},
-            device_id_type=pl.DeviceIdType.MESH,
-        )
-
-    def across(owner, from_src, step, distance, piece):
-        whole = block(me) if from_src else out.at[column, owner]
-        return pltpu.make_async_remote_copy(
-            src_ref=part(whole, piece),
-            dst_ref=part(out.at[column, owner], piece),
-            send_sem=pass_sem.at[step, distance, piece],
-            recv_sem=got_sem.at[step, distance, piece],
-            device_id={"pd": lax.rem(column + step, pd_size)},
-            device_id_type=pl.DeviceIdType.MESH,
-        )
-
-    own = pltpu.make_async_copy(block(me), out.at[column, me], local_sem)
+    def direct(mask, piece):
+        return remote(
+            part(src.at[me ^ mask], piece),
+            part(out.at[column, me], piece),
+            send_sem.at[mask, piece],
+            recv_sem.at[mask, piece],
+            {"ep": me ^ mask},
+        )
+
+    def across(mask, step, piece):
+        return remote(
+            part(src.at[me] if mask == 0 else out.at[column, me ^ mask], piece),
+            part(out.at[column, me ^ mask], piece),
+            pass_sem.at[step, mask, piece],
+            got_sem.at[step, mask, piece],
+            {"pd": lax.rem(column + step, pd_size)},
+        )
+
+    for item in far[:window]:
+        direct(*item).start()
+    for item in near:
+        direct(*item).start()
+    for piece in range(pieces):
+        for step in range(1, pd_size):
+            across(0, step, piece).start()
+    own = pltpu.make_async_copy(src.at[me], out.at[column, me], local_sem)
     own.start()
-    for piece in range(pieces):
-        for step in range(1, pd_size):
-            across(me, True, step, 0, piece).start()
-    for distance in order:
+    for item in interleave(far, near):
+        mask, piece = item
+        direct(*item).wait_recv()
+        if item in far:
+            later = far.index(item) + window
+            direct(*item).wait_send()
+            if later < len(far):
+                direct(*far[later]).start()
+        for step in range(1, pd_size):
+            across(mask, step, piece).start()
+    own.wait()
+    for item in near:
+        direct(*item).wait_send()
+    for mask in range(ep_size):
         for piece in range(pieces):
-            direct(distance, piece).start()
-    for distance in order:
-        for piece in range(pieces):
-            owner = lax.rem(me - distance + ep_size, ep_size)
-            direct(distance, piece).wait_recv()
             for step in range(1, pd_size):
-                across(owner, False, step, distance, piece).start()
-    own.wait()
-    for distance in order:
-        for piece in range(pieces):
-            direct(distance, piece).wait_send()
-    for distance in [0] + order:
-        for piece in range(pieces):
-            owner = lax.rem(me - distance + ep_size, ep_size)
-            for step in range(1, pd_size):
-                copy = across(owner, distance == 0, step, distance, piece)
-                copy.wait_send()
-                copy.wait_recv()
-
-
-def spread(source, block_shape, shared, pieces, collective_id, space):
+                across(mask, step, piece).wait()
+
+
+def spread(source, pieces, window, collective_id):
     ep_size, pd_size = lax.axis_size("ep"), lax.axis_size("pd")
     return pl.pallas_call(
-        functools.partial(spread_kernel, ep_size, pd_size, shared, pieces),
-        out_shape=jax.ShapeDtypeStruct((pd_size, ep_size) + block_shape, source.dtype),
-        in_specs=[pl.BlockSpec(memory_space=space)],
-        out_specs=pl.BlockSpec(memory_space=space),
+        functools.partial(spread_kernel, ep_size, pd_size, pieces, window),
+        out_shape=jax.ShapeDtypeStruct((pd_size,) + source.shape, source.dtype),
+        in_specs=[pl.BlockSpec(memory_space=pl.ANY)],
+        out_specs=pl.BlockSpec(memory_space=pl.ANY),
         scratch_shapes=[
             pltpu.SemaphoreType.DMA,
             pltpu.SemaphoreType.DMA((ep_size, pieces)),
@@ -198,9 +204,162 @@
     )(source)
 
 
+def latent_kernel(
+    ep_size,
+    pd_size,
+    token_rows,
+    slices,
+    weight,
+    gain,
+    out,
+    own_latent,
+    arrived,
+    partial,
+    returned,
+    local_sem,
+    slice_send,
+    slice_recv,
+    part_send,
+    part_recv,
+    send_sem,
+    recv_sem,
+    pass_sem,
+    got_sem,
+    side_send,
+    side_recv,
+):
+    me, column = lax.axis_index("ep"), lax.axis_index("pd")
+    near, far = near_and_far(ep_size)
+    latent_width = gain.shape[-1]
+    meet_peers(ep_size, pd_size)
+
+    def outward(mask):
+        return remote(
+            slices.at[me ^ mask],
+            arrived.at[me],
+            slice_send.at[mask],
+            slice_recv.at[mask],
+            {"ep": me ^ mask},
+        )
+
+    def homeward(mask):
+        return remote(
+            partial.at[me ^ mask],
+            returned.at[me],
+            part_send.at[mask],
+            part_recv.at[mask],
+            {"ep": me ^ mask},
+        )
+
+    for mask in far + near:
+        outward(mask).start()
+    total = jnp.dot(slices[me], weight[...], preferred_element_type=jnp.float32)
+    for mask in near + far:
+        outward(mask).wait_recv()
+        partial[me ^ mask] = jnp.dot(
+            arrived[me ^ mask], weight[...], preferred_element_type=jnp.float32
+        ).astype(jnp.bfloat16)
+        homeward(mask).start()
+    for mask in near + far:
+        homeward(mask).wait_recv()
+        total = total + returned[me ^ mask].astype(jnp.float32)
+    lead = total[:, :latent_width]
+    scale = lax.rsqrt(jnp.mean(lead * lead, axis=-1, keepdims=True) + NORM_EPSILON)
+    own_latent[:, :latent_width] = (lead * scale * gain[...]).astype(jnp.bfloat16)
+    own_latent[:, latent_width:] = total[:, latent_width:].astype(jnp.bfloat16)
+    mine = own_latent.at[pl.ds(0, token_rows)]
+
+    def direct(mask):
+        return remote(
+            mine,
+            out.at[column, me],
+            send_sem.at[mask],
+            recv_sem.at[mask],
+            {"ep": me ^ mask},
+        )
+
+    def across(mask, step):
+        return remote(
+            mine if mask == 0 else out.at[column, me ^ mask],
+            out.at[column, me ^ mask],
+            pass_sem.at[step, mask],
+            got_sem.at[step, mask],
+            {"pd": lax.rem(column + step, pd_size)},
+        )
+
+    def beside(mask, step):
+        origin = lax.rem(column - step + pd_size, pd_size)
+        here = out.at[origin, me ^ mask]
+        return remote(
+            mine if mask == 0 and step == 0 else here,
+            here,
+            side_send.at[step, mask],
+            side_recv.at[step, mask],
+            {"ep": me ^ 1},
+        )
+
+    chips = list(range(2, ep_size, 2))
+    for step in range(1, pd_size):
+        across(0, step).start()
+    for mask in chips[::-1]:
+        direct(mask).start()
+    beside(0, 0).start()
+    own = pltpu.make_async_copy(mine, out.at[column, me], local_sem)
+    own.start()
+    for mask in chips:
+        direct(mask).wait_recv()
+        for step in range(1, pd_size):
+            across(mask, step).start()
+        beside(mask, 0).start()
+    for mask in [0] + chips:
+        for step in range(1, pd_size):
+            across(mask, step).wait_recv()
+            beside(mask, step).start()
+    own.wait()
+    for mask in near + far:
+        outward(mask).wait_send()
+        homeward(mask).wait_send()
+    for mask in chips:
+        direct(mask).wait_send()
+    for mask in [0] + chips:
+        for step in range(pd_size):
+            if step:
+                across(mask, step).wait_send()
+            beside(mask, step).wait()
+
+
+def latents(slices, weight, gain, token_rows, collective_id):
+    ep_size, pd_size = lax.axis_size("ep"), lax.axis_size("pd")
+    rows, width = slices.shape[1], weight.shape[1]
+    vmem = pl.BlockSpec(memory_space=pltpu.VMEM)
+    dma = pltpu.SemaphoreType.DMA
+    return pl.pallas_call(
+        functools.partial(latent_kernel, ep_size, pd_size, token_rows),
+        out_shape=(
+            jax.ShapeDtypeStruct((pd_size, ep_size, token_rows, width), jnp.bfloat16),
+            jax.ShapeDtypeStruct((rows, width), jnp.bfloat16),
+        ),
+        in_specs=[vmem] * 3,
+        out_specs=(vmem, vmem),
+        scratch_shapes=[
+            pltpu.VMEM(slices.shape, jnp.bfloat16),
+            pltpu.VMEM((ep_size, rows, width), jnp.bfloat16),
+            pltpu.VMEM((ep_size, rows, width), jnp.bfloat16),
+            dma,
+            *([dma((ep_size,))] * 6),
+            *([dma((pd_size, ep_size))] * 4),
+        ],
+        compiler_params=pltpu.CompilerParams(
+            collective_id=collective_id, has_side_effects=True, vmem_limit_bytes=48 * 2**20
+        ),
+    )(slices, weight, gain)
+
+
 def collect_kernel(
     ep_size,
     pd_size,
+    pieces,
+    window,
     partial_out,
     out,
     own_rows,
@@ -214,62 +373,65 @@
     recv_sem,
 ):
     me, column = lax.axis_index("ep"), lax.axis_index("pd")
-    order = peer_order(ep_size) + [0]
+    near, far = near_and_far(ep_size)
+    width = out.shape[-1] // pieces
+    items = [(mask, piece) for mask in far + near + [0] for piece in range(pieces)]
     meet_peers(ep_size, pd_size)
 
-    def across(distance, step):
-        target = lax.rem(me + distance, ep_size)
+    def across(mask, piece, step):
+        target = me ^ mask
         there = lax.rem(column + step, pd_size)
-        return pltpu.make_async_remote_copy(
-            src_ref=partial_out.at[there, target],
-            dst_ref=other_rows.at[step - 1, target],
-            send_sem=pass_sem.at[step, distance],
-            recv_sem=got_sem.at[step, distance],
-            device_id={"pd": there},
-            device_id_type=pl.DeviceIdType.MESH,
-        )
-
-    def direct(distance):
-        target = lax.rem(me + distance, ep_size)
-        return pltpu.make_async_remote_copy(
-            src_ref=summed.at[target],
-            dst_ref=out.at[me],
-            send_sem=send_sem.at[distance],
-            recv_sem=recv_sem.at[distance],
-            device_id={"ep": target},
-            device_id_type=pl.DeviceIdType.MESH,
-        )
-
+        columns = pl.ds(piece * width, width)
+        return remote(
+            partial_out.at[there, target, :, columns],
+            other_rows.at[step - 1, target, :, columns],
+            pass_sem.at[step, mask, piece],
+            got_sem.at[step, mask, piece],
+            {"pd": there},
+        )
+
+    def direct(mask, piece):
+        columns = pl.ds(piece * width, width)
+        return remote(
+            summed.at[me ^ mask, :, columns],
+            out.at[me, :, columns],
+            send_sem.at[mask, piece],
+            recv_sem.at[mask, piece],
+            {"ep": me ^ mask},
+        )
+
+    for item in items[:window]:
+        for step in range(1, pd_size):
+            across(*item, step).start()
     fetch = pltpu.make_async_copy(partial_out.at[column], own_rows, own_sem)
     fetch.start()
-    for distance in order:
-        for step in range(1, pd_size):
-            across(distance, step).start()
     fetch.wait()
-    for distance in order:
-        target = lax.rem(me + distance, ep_size)
-        total = own_rows[target].astype(jnp.float32)
-        for step in range(1, pd_size):
-            across(distance, step).wait_recv()
-            total = total + other_rows[step - 1, target].astype(jnp.float32)
-        summed[target] = total.astype(jnp.bfloat16)
-        if distance:
-            direct(distance).start()
+    for at, item in enumerate(items):
+        mask, piece = item
+        target = me ^ mask
+        columns = pl.ds(piece * width, width)
+        for step in range(1, pd_size):
+            across(*item, step).wait()
+            if at + window < len(items):
+                across(*items[at + window], step).start()
+        total = own_rows[target, :, columns].astype(jnp.float32)
+        for step in range(1, pd_size):
+            total = total + other_rows[step - 1, target, :, columns].astype(jnp.float32)
+        summed[target, :, columns] = total.astype(jnp.bfloat16)
+        if mask:
+            direct(*item).start()
     keep = pltpu.make_async_copy(summed.at[me], out.at[me], local_sem)
     keep.start()
-    for distance in order:
-        for step in range(1, pd_size):
-            across(distance, step).wait_send()
-        if distance:
-            direct(distance).wait_send()
-            direct(distance).wait_recv()
+    for mask, piece in items:
+        if mask:
+            direct(mask, piece).wait()
     keep.wait()
 
 
-def collect(partial_out, collective_id):
+def collect(partial_out, pieces, window, collective_id):
     pd_size, ep_size, capacity, width = partial_out.shape
     return pl.pallas_call(
-        functools.partial(collect_kernel, ep_size, pd_size),
+        functools.partial(collect_kernel, ep_size, pd_size, pieces, window),
         out_shape=jax.ShapeDtypeStruct((ep_size, capacity, width), jnp.bfloat16),
         in_specs=[pl.BlockSpec(memory_space=pl.ANY)],
         out_specs=pl.BlockSpec(memory_space=pl.ANY),
@@ -279,10 +441,10 @@
             pltpu.VMEM((ep_size, capacity, width), jnp.bfloat16),
             pltpu.SemaphoreType.DMA,
             pltpu.SemaphoreType.DMA,
-            pltpu.SemaphoreType.DMA((pd_size, ep_size)),
-            pltpu.SemaphoreType.DMA((pd_size, ep_size)),
-            pltpu.SemaphoreType.DMA((ep_size,)),
-            pltpu.SemaphoreType.DMA((ep_size,)),
+            pltpu.SemaphoreType.DMA((pd_size, ep_size, pieces)),
+            pltpu.SemaphoreType.DMA((pd_size, ep_size, pieces)),
+            pltpu.SemaphoreType.DMA((ep_size, pieces)),
+            pltpu.SemaphoreType.DMA((ep_size, pieces)),
         ],
         compiler_params=pltpu.CompilerParams(
             collective_id=collective_id, has_side_effects=True, vmem_limit_bytes=48 * 2**20
@@ -332,7 +494,7 @@
     )
     gate_local = gate_up[0]
     down_local = down_proj[0]
-    arrived = spread(outgoing, (capacity, model_width), False, 2, 1, pl.ANY)
+    arrived = spread(outgoing, 2, 2, 1)
     row_block = arrived.reshape(-1, model_width)
     gate_val = jnp.einsum("rd,dgf->rgf", row_block, gate_local, preferred_element_type=jnp.float32)
     partial_value = jnp.dot(
@@ -341,7 +503,7 @@
         preferred_element_type=jnp.float32,
     ).astype(jnp.bfloat16)
     partial_out = partial_value.reshape(arrived.shape)
-    expert_out = collect(partial_out, 2).reshape(-1, model_width)
+    expert_out = collect(partial_out, 2, 2, 2).reshape(-1, model_width)
     mix_high = mix.astype(jnp.bfloat16)
     mix_low = (mix - mix_high.astype(jnp.float32)).astype(jnp.bfloat16)
     both = jnp.einsum(
@@ -361,22 +523,14 @@
         ),
         attn_gain,
     ).astype(jnp.bfloat16)
-    all_rows = kv_input.shape[0]
-    slices = kv_input.reshape(all_rows, experts, -1).swapaxes(0, 1)
-    gathered = lax.all_to_all(slices, "ep", split_axis=0, concat_axis=0, tiled=True)
-    pieces = jnp.einsum(
-        "erk,kl->erl", gathered, kv_weight, preferred_element_type=jnp.float32
-    ).astype(jnp.bfloat16)
-    compressed = jnp.sum(
-        lax.all_to_all(pieces, "ep", split_axis=0, concat_axis=0, tiled=True),
-        axis=0,
-        dtype=jnp.float32,
-    )
-    latent_all = jnp.concatenate(
-        [rms_norm(compressed[:, :latent_width], kv_gain), compressed[:, latent_width:]], axis=-1
-    ).astype(jnp.bfloat16)
-    prompt_latent = latent_all[:tok_rows]
-    draft_latent = latent_all[tok_rows:].reshape(slot_count, step_count, row_width)
+    spare = -kv_input.shape[0] % 16
+    slices = (
+        jnp.pad(kv_input, ((0, spare), (0, 0))).reshape(-1, experts, kv_weight.shape[0])
+    ).swapaxes(0, 1)
+    shard_rows, own_latent = latents(slices, kv_weight, kv_gain[None], tok_rows, 3)
+    draft_latent = own_latent[tok_rows : tok_rows + slot_count * step_count].reshape(
+        slot_count, step_count, row_width
+    )
     device = lax.axis_index(("ep", "pd"))
     slot_ids = device * slot_count + jnp.arange(slot_count, dtype=jnp.int32)
     owner_hit = assign[None, :] == slot_ids[:, None]
@@ -388,9 +542,7 @@
     block_ids = jnp.arange(block_cap, dtype=jnp.int32)
     wanted = first_row[:, None] + block_ids[None, :]
     live_rows = block_ids[None, :] < block_len[:, None]
-    shard_rows = spread(prompt_latent, prompt_latent.shape, True, 1, 3, pltpu.VMEM).reshape(
-        -1, row_width
-    )
+    shard_rows = shard_rows.reshape(-1, row_width)
     places = jnp.arange(quarters * experts * tok_rows, dtype=jnp.int32)
     from_pd, from_ep = places // (experts * tok_rows), places // tok_rows % experts
     row_index = (from_ep * quarters + from_pd) * tok_rows + places % tok_rows

time: 333 us -> 301 us (0.904)
  waiting for transfers between devices: 36.7 us -> 0 us
  Pallas kernels: 236 us -> 252 us
  starting transfers between devices: 10.4 us -> 0 us
    all_to_all x2 -> x0, waiting for transfers between devices: 36.7 us -> none  [the longest x1 23 us: per_device(): lax.all_to_all(slices, 'ep', split_axis=0, concat_axis=0, tiled=True)]
    pallas_call x3, Pallas kernels: 236 us -> 252 us  [the longest x1 99.1 us: collect(): pl.pallas_call(functools.partial(collect_kernel, ep_size, pd_size, pieces...]
    all_to_all x2 -> x0, starting transfers between devices: 10.4 us -> none  [the longest x1 6.59 us: per_device(): lax.all_to_all(slices, 'ep', split_axis=0, concat_axis=0, tiled=True)]
  transfers between devices with their start and end apart: 2 -> 0, of which waited for: 2 -> 0; matrix products, arithmetic and copies ran while one was open for 2% -> 0% of each run, Pallas kernels for 0% -> 0%
where the time goes in v2:
time: 301 us
  Pallas kernels  252 us (84%)
  matrix products  26 us (9%)
  local copies, waits for them, and re-layouts  12.8 us (4%)
  other arithmetic  7.89 us (3%)
    pallas_call x1, Pallas kernels, collect(): pl.pallas_call(functools.partial(collect_kernel, ep_size, pd_size, pieces...  99.1 us
    pallas_call x1, Pallas kernels, spread(): pl.pallas_call(functools.partial(spread_kernel, ep_size, pd_size, pieces,...  88.5 us
    pallas_call x1, Pallas kernels, latents(): pl.pallas_call(functools.partial(latent_kernel, ep_size, pd_size, token_r...  64 us
    dot_general x1, matrix products, per_device(): jnp.einsum('rd,dgf->rgf', row_block, gate_local, preferred_element_type=j...  11.3 us
    unnamed x35, local copies, waits for them, and re-layouts  6.64 us
    dot_general x1, matrix products, per_device(): jnp.dot((jax.nn.silu(gate_val[:, 0]) * gate_val[:, 1]).astype(jnp.bfloat1...  6.06 us

profile of v2, /device:TPU:0, one launch (start us, length us, event | category | flops | bytes accessed | tf_op | source)
XLA Modules:
  0.0 300.9 jit_solution(6627355313033701301)
XLA Ops:
  0.6 0.8 copy.80
  1.4 0.1 eq.70
  1.5 0.1 fusion.67
  1.6 0.2 reduce_window_sum.18
  1.8 0.2 select_reduce_fusion.1
  2.0 0.1 reduce_sum.77
  2.1 0.1 copy.81
  2.2 0.7 multiply_add_fusion
  2.9 0.1 fusion.55
  3.0 1.5 fusion.6
  4.5 2.4 convolution_convert_fusion.1
  6.8 0.0 slice-start
  6.9 88.5 %shard_map.158 = bf16[2,8,32,7168]{3,2,1,0:T(8,128)(2,1)S(1)} custom-call(bf16[8,32,7168]{2,1,0:T(8,128)(2,1)S(1)} %bitcast.76), custom_call_target="tpu_custom_call" | custom-call | tf_op jit(solution)/shard_map/pallas_call | solution.py:189
  95.4 0.0 slice-start.1
  95.4 11.3 %fusion = f32[512,2,512]{2,0,1:T(8,128)S(1)} fusion(bf16[512,7168,1]{1,0,2:T(8,128)(2,1)S(1)} %bitcast.77, bf16[7168,2,512]{2,1,0:T(2,128)(2,1)} %bitcast.95), kind=kOutput, calls=%fused_computation | convolution fusion | flops 7516192768 | bytes 24117248 | tf_op jit(solution)/shard_map/rd,dgf->rgf/dot_general | solution.py:499
  106.8 6.1 %convolution_convert_fusion = bf16[512,7168]{1,0:T(8,128)(2,1)} fusion(bf16[1,512,7168]{2,1,0:T(8,128)(2,1)S(1)} %bitcast.97, f32[512,2,512]{2,0,1:T(8,128)S(1)} %fusion), kind=kOutput, calls=%fused_computation.2 | convolution fusion | flops 3763339264 | bytes 16777216 | tf_op jit(solution)/shard_map/dot_general | solution.py:500
  112.8 99.1 %shard_map.159 = bf16[8,32,7168]{2,1,0:T(8,128)(2,1)S(1)} custom-call(bf16[2,8,32,7168]{3,2,1,0:T(8,128)(2,1)} %bitcast.81), custom_call_target="tpu_custom_call" | custom-call | tf_op jit(solution)/shard_map/pallas_call | solution.py:433
  211.9 1.8 copy-done
  213.7 0.1 select_reduce_fusion
  213.9 2.8 fusion.62
  216.6 0.0 copy-start.12
  216.6 0.0 copy-start.13
  216.7 0.2 fusion.9
  216.9 0.0 copy-start.3
  216.9 0.4 copy-done.12
  217.3 0.1 copy.86
  217.4 0.1 reduce.6
  217.5 0.7 fusion.95
  218.3 0.7 iota_compare_fusion.4
  219.6 0.1 pad_add_fusion
  219.7 0.1 broadcast_in_dim.38
  219.8 0.4 copy.93
  220.2 1.2 slice.61
  221.3 1.1 slice.60
  223.2 0.2 fusion.61
  223.4 0.1 copy.83
  223.5 0.1 copy.84
  223.7 0.8 pad_maximum_fusion.1
  224.4 0.3 fusion.3
  224.8 0.3 fusion.5
  225.1 0.1 pad.4
  225.2 0.1 copy.99
  225.3 1.0 copy-done.5
  226.3 1.3 copy.88.weight
  227.6 64.0 %shard_map.160 = (bf16[2,8,64,576]{3,2,1,0:T(8,128)(2,1)S(1)}, bf16[80,576]{1,0:T(8,128)(2,1)S(1)}) custom-call(bf16[8,80,896]{2,1,0:T(8,128)(2,1)S(1)} %bitcast.78, bf16[896,576]{1,0:T(8,128)(2,1)S(1)} %copy.88.weight, f32[1,512]{1,0:T(1,128)S(1)} %bitcast.79), custom_call_target="tpu_custom_call" | custom-call | tf_op jit(solution)/shard_map/pallas_call | solution.py:336
  291.7 1.1 copy-done.2
  292.7 0.1 slice.69
  292.9 0.1 slice.68
  293.0 0.1 fusion.93
  293.1 0.1 copy.91
  293.2 0.1 copy.92
  293.4 0.7 iota_add_fusion
  294.0 1.9 convolution_convert_fusion.3
  295.9 0.9 slice.65
  296.8 0.9 slice.64
  297.7 0.4 fusion.69
  298.2 0.1 copy.89
  298.3 0.1 copy.90
  298.5 0.3 copy.85
  298.8 0.5 fusion.100
  299.3 0.2 fusion.37
  299.5 0.1 divide_convert_fusion
  299.6 0.2 copy.94
  299.8 1.1 fusion.12
  (47 shorter events, 0.4 us)
Async XLA Ops:
  6.8 99.9 %slice-start = ((s8[7340032]{0:T(1024)(128)(4,1)}), s8[4194304]{0:T(1024)(128)(4,1)S(1)}, s32[]{:S(2)}) async-start(s8[7340032]{0:T(1024)(128)(4,1)} %bitcast.96), calls=%async_computation | async-start | bytes 8388608
  95.4 11.4 %slice-start.1 = ((s8[7340032]{0:T(1024)(128)(4,1)}), s8[3145728]{0:T(1024)(128)(4,1)S(1)}, s32[]{:S(2)}) async-start(s8[7340032]{0:T(1024)(128)(4,1)} %bitcast.96), calls=%async_computation.1 | async-start | bytes 6291456
  112.8 100.9 %copy-start.11 = (f32[64,2]{0,1:T(2,128)S(1)}, f32[64,2]{0,1:T(2,128)}, u32[]{:S(2)}) copy-start(f32[64,2]{0,1:T(2,128)} %param.18) | copy-start | bytes 1540
  211.9 1.8 copy-start
  213.8 2.8 copy-start.4
  216.6 0.7 copy-start.12
  216.6 0.9 copy-start.13
  216.7 3.5 %copy-start.7 = (bf16[1,4,64,576]{3,2,1,0:T(8,128)(2,1)S(1)}, bf16[1,4,64,576]{3,2,1,0:T(8,128)(2,1)}, u32[]{:S(2)}) copy-start(bf16[1,4,64,576]{3,2,1,0:T(8,128)(2,1)} %param.29) | copy-start | bytes 884740
  216.9 7.9 %copy-start.3 = (bf16[64,7168]{1,0:T(8,128)(2,1)}, bf16[64,7168]{1,0:T(8,128)(2,1)S(1)}, u32[]{:S(2)}) copy-start(bf16[64,7168]{1,0:T(8,128)(2,1)S(1)} %fusion.9) | copy-start | bytes 2752516
  216.9 7.5 %copy-start.9 = (bf16[1,4,7168]{2,1,0:T(4,128)(2,1)S(1)}, bf16[1,4,7168]{2,1,0:T(4,128)(2,1)}, u32[]{:S(2)}) copy-start(bf16[1,4,7168]{2,1,0:T(4,128)(2,1)} %param.28) | copy-start | bytes 172036
  219.8 5.0 %copy-start.10 = (f32[7168]{0:T(1024)S(1)}, f32[7168]{0:T(1024)}, u32[]{:S(2)}) copy-start(f32[7168]{0:T(1024)} %param.22) | copy-start | bytes 86020
  225.1 1.2 copy-start.5
  225.2 2.4 copy-start.1
  291.7 1.1 copy-start.2
  292.7 5.7 %copy-start.6 = (bf16[1,512,576]{1,2,0:T(8,128)(2,1)S(1)}, bf16[1,512,576]{1,2,0:T(8,128)(2,1)}, u32[]{:S(2)}) copy-start(bf16[1,512,576]{1,2,0:T(8,128)(2,1)} %param.26) | copy-start | bytes 1769476
  294.0 4.8 %copy-start.8 = (bf16[4,64,576]{2,1,0:T(8,128)(2,1)S(1)}, bf16[4,64,576]{2,1,0:T(8,128)(2,1)}, u32[]{:S(2)}) copy-start(bf16[4,64,576]{2,1,0:T(8,128)(2,1)} %pad_maximum_fusion.1) | copy-start | bytes 884740

commit v3 on v2

--- a/solution.py
+++ b/solution.py
@@ -22,19 +22,15 @@
 def with_rope(row_vals, positions, rotary_width):
     latent_width = row_vals.shape[-1] - rotary_width
     rotary = row_vals[..., latent_width:].astype(jnp.float32)
-    frequency = ROPE_BASE ** (
-        -jnp.arange(rotary_width // 2, dtype=jnp.float32) * 2.0 / rotary_width
-    )
+    lane = jnp.arange(rotary_width, dtype=jnp.int32)
+    frequency = ROPE_BASE ** (-(lane // 2).astype(jnp.float32) * 2.0 / rotary_width)
     angles = positions.astype(jnp.float32)[..., None] * frequency
-    even_part = rotary[..., 0::2]
-    odd_part = rotary[..., 1::2]
-    turned = jnp.stack(
-        [
-            even_part * jnp.cos(angles) - odd_part * jnp.sin(angles),
-            even_part * jnp.sin(angles) + odd_part * jnp.cos(angles),
-        ],
-        axis=-1,
-    ).reshape(rotary.shape)
+    pair = lane[:, None] == (lane ^ 1)[None, :]
+    swap = jnp.where(pair, jnp.where(lane % 2 == 0, -1.0, 1.0)[None, :], 0.0).astype(jnp.bfloat16)
+    partner = jnp.dot(
+        row_vals[..., latent_width:], swap, preferred_element_type=jnp.float32
+    )
+    turned = rotary * jnp.cos(angles) + partner * jnp.sin(angles)
     return jnp.concatenate([row_vals[..., :latent_width], turned.astype(jnp.bfloat16)], axis=-1)
 
 
@@ -53,8 +49,7 @@
         ],
         axis=0,
     )
-    head_pos = jnp.broadcast_to(draft_pos[:, None], (step_count, head_count))
-    turned_query = with_rope(query, head_pos, rotary_width).reshape(
+    turned_query = with_rope(query, draft_pos[:, None], rotary_width).reshape(
         step_count * head_count, row_width
     )
     live_cache = jnp.broadcast_to(
@@ -126,7 +121,22 @@
 
 
 def spread_kernel(
-    ep_size, pd_size, pieces, window, src, out, local_sem, send_sem, recv_sem, pass_sem, got_sem
+    ep_size,
+    pd_size,
+    pieces,
+    window,
+    src,
+    weight,
+    out,
+    weight_pair,
+    local_sem,
+    weight_sem,
+    pair_send,
+    pair_recv,
+    send_sem,
+    recv_sem,
+    pass_sem,
+    got_sem,
 ):
     me, column = lax.axis_index("ep"), lax.axis_index("pd")
     width = out.shape[-1] // pieces
@@ -165,6 +175,11 @@
             across(0, step, piece).start()
     own = pltpu.make_async_copy(src.at[me], out.at[column, me], local_sem)
     own.start()
+    core = lax.rem(me, 2)
+    keep = pltpu.make_async_copy(weight, weight_pair.at[core], weight_sem)
+    keep.start()
+    give = remote(weight, weight_pair.at[core], pair_send, pair_recv, {"ep": me ^ 1})
+    give.start()
     for item in interleave(far, near):
         mask, piece = item
         direct(*item).wait_recv()
@@ -176,6 +191,8 @@
         for step in range(1, pd_size):
             across(mask, step, piece).start()
     own.wait()
+    keep.wait()
+    give.wait()
     for item in near:
         direct(*item).wait_send()
     for mask in range(ep_size):
@@ -184,15 +201,18 @@
                 across(mask, step, piece).wait()
 
 
-def spread(source, pieces, window, collective_id):
+def spread(source, weight, pieces, window, collective_id):
     ep_size, pd_size = lax.axis_size("ep"), lax.axis_size("pd")
     return pl.pallas_call(
         functools.partial(spread_kernel, ep_size, pd_size, pieces, window),
-        out_shape=jax.ShapeDtypeStruct((pd_size,) + source.shape, source.dtype),
-        in_specs=[pl.BlockSpec(memory_space=pl.ANY)],
-        out_specs=pl.BlockSpec(memory_space=pl.ANY),
+        out_shape=(
+            jax.ShapeDtypeStruct((pd_size,) + source.shape, source.dtype),
+            jax.ShapeDtypeStruct((2,) + weight.shape, weight.dtype),
+        ),
+        in_specs=[pl.BlockSpec(memory_space=pl.ANY)] * 2,
+        out_specs=(pl.BlockSpec(memory_space=pl.ANY),) * 2,
         scratch_shapes=[
-            pltpu.SemaphoreType.DMA,
+            *([pltpu.SemaphoreType.DMA] * 4),
             pltpu.SemaphoreType.DMA((ep_size, pieces)),
             pltpu.SemaphoreType.DMA((ep_size, pieces)),
             pltpu.SemaphoreType.DMA((pd_size, ep_size, pieces)),
@@ -201,7 +221,7 @@
         compiler_params=pltpu.CompilerParams(
             collective_id=collective_id, has_side_effects=True, vmem_limit_bytes=40 * 2**20
         ),
-    )(source)
+    )(source, weight)
 
 
 def latent_kernel(
@@ -229,14 +249,20 @@
     side_recv,
 ):
     me, column = lax.axis_index("ep"), lax.axis_index("pd")
-    near, far = near_and_far(ep_size)
+    here = lax.div(me, 2)
+    chips = list(range(2, ep_size, 2))
+    near = [mask for mask in chips if 2 * mask < ep_size]
+    far = [mask for mask in chips if 2 * mask >= ep_size]
     latent_width = gain.shape[-1]
     meet_peers(ep_size, pd_size)
 
+    def chip(mask):
+        return lax.div(me ^ mask, 2)
+
     def outward(mask):
         return remote(
-            slices.at[me ^ mask],
-            arrived.at[me],
+            slices.at[chip(mask)],
+            arrived.at[here],
             slice_send.at[mask],
             slice_recv.at[mask],
             {"ep": me ^ mask},
@@ -244,25 +270,29 @@
 
     def homeward(mask):
         return remote(
-            partial.at[me ^ mask],
-            returned.at[me],
+            partial.at[chip(mask)],
+            returned.at[here],
             part_send.at[mask],
             part_recv.at[mask],
             {"ep": me ^ mask},
         )
 
-    for mask in far + near:
+    for mask in far[:1] + near:
         outward(mask).start()
-    total = jnp.dot(slices[me], weight[...], preferred_element_type=jnp.float32)
-    for mask in near + far:
-        outward(mask).wait_recv()
-        partial[me ^ mask] = jnp.dot(
-            arrived[me ^ mask], weight[...], preferred_element_type=jnp.float32
-        ).astype(jnp.bfloat16)
-        homeward(mask).start()
-    for mask in near + far:
+    total = jnp.dot(slices[here], weight[...], preferred_element_type=jnp.float32)
+    for at, mask in enumerate(far):
+        outward(mask).wait_send()
+        for later in far[at + 1 : at + 2]:
+            outward(later).start()
+        for ready in [mask] if at else near + [mask]:
+            outward(ready).wait_recv()
+            partial[chip(ready)] = jnp.dot(
+                arrived[chip(ready)], weight[...], preferred_element_type=jnp.float32
+            ).astype(jnp.bfloat16)
+            homeward(ready).start()
+    for mask in chips:
         homeward(mask).wait_recv()
-        total = total + returned[me ^ mask].astype(jnp.float32)
+        total = total + returned[chip(mask)].astype(jnp.float32)
     lead = total[:, :latent_width]
     scale = lax.rsqrt(jnp.mean(lead * lead, axis=-1, keepdims=True) + NORM_EPSILON)
     own_latent[:, :latent_width] = (lead * scale * gain[...]).astype(jnp.bfloat16)
@@ -298,7 +328,6 @@
             {"ep": me ^ 1},
         )
 
-    chips = list(range(2, ep_size, 2))
     for step in range(1, pd_size):
         across(0, step).start()
     for mask in chips[::-1]:
@@ -316,10 +345,10 @@
             across(mask, step).wait_recv()
             beside(mask, step).start()
     own.wait()
-    for mask in near + far:
+    for mask in near:
         outward(mask).wait_send()
+    for mask in chips:
         homeward(mask).wait_send()
-    for mask in chips:
         direct(mask).wait_send()
     for mask in [0] + chips:
         for step in range(pd_size):
@@ -343,8 +372,8 @@
         out_specs=(vmem, vmem),
         scratch_shapes=[
             pltpu.VMEM(slices.shape, jnp.bfloat16),
-            pltpu.VMEM((ep_size, rows, width), jnp.bfloat16),
-            pltpu.VMEM((ep_size, rows, width), jnp.bfloat16),
+            pltpu.VMEM((ep_size // 2, rows, width), jnp.bfloat16),
+            pltpu.VMEM((ep_size // 2, rows, width), jnp.bfloat16),
             dma,
             *([dma((ep_size,))] * 6),
             *([dma((pd_size, ep_size))] * 4),
@@ -494,7 +523,7 @@
     )
     gate_local = gate_up[0]
     down_local = down_proj[0]
-    arrived = spread(outgoing, 2, 2, 1)
+    arrived, weight_pair = spread(outgoing, kv_weight, 4, 4, 1)
     row_block = arrived.reshape(-1, model_width)
     gate_val = jnp.einsum("rd,dgf->rgf", row_block, gate_local, preferred_element_type=jnp.float32)
     partial_value = jnp.dot(
@@ -503,7 +532,7 @@
         preferred_element_type=jnp.float32,
     ).astype(jnp.bfloat16)
     partial_out = partial_value.reshape(arrived.shape)
-    expert_out = collect(partial_out, 2, 2, 2).reshape(-1, model_width)
+    expert_out = collect(partial_out, 4, 6, 2).reshape(-1, model_width)
     mix_high = mix.astype(jnp.bfloat16)
     mix_low = (mix - mix_high.astype(jnp.float32)).astype(jnp.bfloat16)
     both = jnp.einsum(
@@ -525,9 +554,11 @@
     ).astype(jnp.bfloat16)
     spare = -kv_input.shape[0] % 16
     slices = (
-        jnp.pad(kv_input, ((0, spare), (0, 0))).reshape(-1, experts, kv_weight.shape[0])
+        jnp.pad(kv_input, ((0, spare), (0, 0))).reshape(-1, experts // 2, 2 * kv_weight.shape[0])
     ).swapaxes(0, 1)
-    shard_rows, own_latent = latents(slices, kv_weight, kv_gain[None], tok_rows, 3)
+    shard_rows, own_latent = latents(
+        slices, weight_pair.reshape(-1, row_width), kv_gain[None], tok_rows, 3
+    )
     draft_latent = own_latent[tok_rows : tok_rows + slot_count * step_count].reshape(
         slot_count, step_count, row_width
     )

time: 301 us -> 287 us (0.953)
  Pallas kernels: 252 us -> 240 us
  local copies, waits for them, and re-layouts: 12.8 us -> 9.54 us
    pallas_call x1, Pallas kernels: 64 us -> 52.8 us  [latents(): pl.pallas_call(functools.partial(latent_kernel, ep_size, pd_size, token_r...]
    slice x6 -> x0, local copies, waits for them, and re-layouts: 4.27 us -> none  [the longest x3 2.16 us: with_rope(): odd_part = rotary[..., 1::2]]
where the time goes in v3:
time: 287 us
  Pallas kernels  240 us (84%)
  matrix products  28.6 us (10%)
  local copies, waits for them, and re-layouts  9.54 us (3%)
  other arithmetic  6.38 us (2%)
    pallas_call x1, Pallas kernels, collect(): pl.pallas_call(functools.partial(collect_kernel, ep_size, pd_size, pieces...  97.7 us
    pallas_call x1, Pallas kernels, spread(): pl.pallas_call(functools.partial(spread_kernel, ep_size, pd_size, pieces,...  89.3 us
    pallas_call x1, Pallas kernels, latents(): pl.pallas_call(functools.partial(latent_kernel, ep_size, pd_size, token_r...  52.8 us
    dot_general x1, matrix products, per_device(): jnp.einsum('rd,dgf->rgf', row_block, gate_local, preferred_element_type=j...  11.3 us
    unnamed x35, local copies, waits for them, and re-layouts  8.14 us
    dot_general x1, matrix products, per_device(): jnp.dot((jax.nn.silu(gate_val[:, 0]) * gate_val[:, 1]).astype(jnp.bfloat1...  6.06 us

profile of v3, /device:TPU:0, one launch (start us, length us, event | category | flops | bytes accessed | tf_op | source)
XLA Modules:
  0.0 286.8 jit_solution(13509872783190030917)
XLA Ops:
  0.6 0.8 copy.51
  1.4 0.1 eq.126
  1.5 0.1 fusion.54
  1.6 0.2 reduce_window_sum.18
  1.8 0.2 select_reduce_fusion.1
  2.0 0.1 reduce_sum.77
  2.1 0.1 copy.52
  2.2 0.7 multiply_add_fusion
  2.9 0.1 fusion.46
  3.0 1.5 fusion.6
  4.5 0.0 copy-start.6
  4.5 4.3 %convolution_convert_fusion.1 = bf16[256,7168]{1,0:T(8,128)(2,1)} fusion(pred[256,64]{0,1:T(8,128)(4,1)S(1)} %fusion.46, bf16[64,7168]{1,0:T(8,128)(2,1)} %param.15, f32[7168]{0:T(1024)} %param.16, f32[64]{0:T(128)S(1)} %add_rsqrt_fusion.1), kind=kOutput, calls=%fused_computation.3 | convolution fusion | flops 238551040 | bytes 4632832 | tf_op jit(solution)/shard_map/dot_general | solution.py:520
  8.7 1.1 copy.53.weight
  9.8 0.0 copy-start
  9.9 2.0 copy-done
  11.9 89.3 %shard_map.158 = (bf16[2,8,32,7168]{3,2,1,0:T(8,128)(2,1)S(1)}, bf16[2,896,576]{2,1,0:T(8,128)(2,1)S(1)}) custom-call(bf16[8,32,7168]{2,1,0:T(8,128)(2,1)S(1)} %bitcast.71, bf16[896,576]{1,0:T(8,128)(2,1)S(1)} %copy.53.weight), custom_call_target="tpu_custom_call" | custom-call | tf_op jit(solution)/shard_map/pallas_call | solution.py:206
  101.2 0.0 slice-start.1
  101.3 11.3 %fusion = f32[512,2,512]{2,0,1:T(8,128)S(1)} fusion(bf16[512,7168,1]{1,0,2:T(8,128)(2,1)S(1)} %bitcast.76, bf16[7168,2,512]{2,1,0:T(2,128)(2,1)} %bitcast.90), kind=kOutput, calls=%fused_computation | convolution fusion | flops 7516192768 | bytes 24117248 | tf_op jit(solution)/shard_map/rd,dgf->rgf/dot_general | solution.py:528
  112.6 6.1 %convolution_convert_fusion = bf16[512,7168]{1,0:T(8,128)(2,1)} fusion(bf16[1,512,7168]{2,1,0:T(8,128)(2,1)S(1)} %bitcast.92, f32[512,2,512]{2,0,1:T(8,128)S(1)} %fusion), kind=kOutput, calls=%fused_computation.2 | convolution fusion | flops 3763339264 | bytes 16777216 | tf_op jit(solution)/shard_map/dot_general | solution.py:529
  118.7 97.7 %shard_map.159 = bf16[8,32,7168]{2,1,0:T(8,128)(2,1)S(1)} custom-call(bf16[2,8,32,7168]{3,2,1,0:T(8,128)(2,1)} %bitcast.78), custom_call_target="tpu_custom_call" | custom-call | tf_op jit(solution)/shard_map/pallas_call | solution.py:462
  216.4 1.8 copy-done.1
  218.2 0.0 copy-done.11
  218.2 0.1 select_reduce_fusion
  218.3 0.0 copy-start.5
  218.3 2.8 fusion.49
  221.1 0.0 copy-done.5
  221.1 0.0 copy-start.8
  221.1 0.0 copy-start.10
  221.1 0.2 fusion.9
  221.4 0.0 copy-start.4
  221.4 0.6 copy-done.8
  221.9 0.3 fusion.3
  222.3 0.3 fusion.5
  222.6 0.0 copy-start.2
  222.6 0.1 pad.4
  222.7 0.1 copy.67
  222.8 0.0 copy-start.12
  222.8 0.0 copy-start.13
  222.8 0.5 copy-done.2
  223.3 52.8 %shard_map.160 = (bf16[2,8,64,576]{3,2,1,0:T(8,128)(2,1)S(1)}, bf16[80,576]{1,0:T(8,128)(2,1)S(1)}) custom-call(bf16[4,80,1792]{2,1,0:T(8,128)(2,1)S(1)} %bitcast.73, bf16[1792,576]{1,0:T(8,128)(2,1)S(1)} %bitcast.74, f32[1,512]{1,0:T(1,128)S(1)} %bitcast.75), custom_call_target="tpu_custom_call" | custom-call | tf_op jit(solution)/shard_map/pallas_call | solution.py:365
  276.1 0.0 copy-start.3
  276.1 1.1 copy-done.3
  277.2 0.1 copy.56
  277.3 0.1 reduce.6
  277.4 0.7 fusion.87
  278.1 0.6 iota_compare_fusion.5
  278.7 0.7 iota_add_fusion
  279.4 2.0 convolution_convert_fusion.2
  281.4 0.0 copy-start.7
  282.2 0.3 fusion.17
  282.6 0.2 copy.59
  283.4 0.1 fusion.19
  283.5 0.1 multiply_cosine_fusion.1
  283.6 0.2 fusion.15
  283.9 0.1 pad_add_fusion
  284.0 0.1 broadcast_in_dim.126
  284.0 0.4 copy.60
  284.4 0.0 copy-done.7
  284.4 0.3 copy.55
  284.7 0.5 fusion.95
  285.2 0.2 fusion.40
  285.4 0.1 divide_convert_fusion
  285.5 0.2 copy.61
  285.7 1.1 fusion.12
  (33 shorter events, 0.3 us)
Async XLA Ops:
  4.5 4.3 %copy-start.6 = (bf16[896,576]{0,1:T(8,128)(2,1)S(1)}, bf16[896,576]{0,1:T(8,128)(2,1)}, u32[]{:S(2)}) copy-start(bf16[896,576]{0,1:T(8,128)(2,1)} %param.21) | copy-start | bytes 3096580
  9.8 2.0 copy-start
  11.9 100.7 %slice-start = ((s8[7340032]{0:T(1024)(128)(4,1)}), s8[4194304]{0:T(1024)(128)(4,1)S(1)}, s32[]{:S(2)}) async-start(s8[7340032]{0:T(1024)(128)(4,1)} %bitcast.91), calls=%async_computation | async-start | bytes 8388608
  101.2 11.4 %slice-start.1 = ((s8[7340032]{0:T(1024)(128)(4,1)}), s8[3145728]{0:T(1024)(128)(4,1)S(1)}, s32[]{:S(2)}) async-start(s8[7340032]{0:T(1024)(128)(4,1)} %bitcast.91), calls=%async_computation.1 | async-start | bytes 6291456
  118.7 99.5 %copy-start.11 = (f32[64,2]{0,1:T(2,128)S(1)}, f32[64,2]{0,1:T(2,128)}, u32[]{:S(2)}) copy-start(f32[64,2]{0,1:T(2,128)} %param.18) | copy-start | bytes 1540
  216.4 1.8 copy-start.1
  218.3 2.8 copy-start.5
  221.1 0.8 copy-start.8
  221.1 1.1 copy-start.10
  221.4 1.3 copy-start.4
  222.6 0.7 copy-start.2
  222.8 54.4 %copy-start.12 = (s32[16]{0:T(128)S(1)}, s32[16]{0:T(128)}, u32[]{:S(2)}) copy-start(s32[16]{0:T(128)} %param.24) | copy-start | bytes 196
  222.8 54.6 %copy-start.13 = (s32[16]{0:T(128)S(1)}, s32[16]{0:T(128)}, u32[]{:S(2)}) copy-start(s32[16]{0:T(128)} %param.25) | copy-start | bytes 196
  276.1 1.1 copy-start.3
  277.1 6.5 %copy-start.9 = (bf16[1,4,64,576]{3,2,1,0:T(8,128)(2,1)S(1)}, bf16[1,4,64,576]{3,2,1,0:T(8,128)(2,1)}, u32[]{:S(2)}) copy-start(bf16[1,4,64,576]{3,2,1,0:T(8,128)(2,1)} %param.29) | copy-start | bytes 884740
  281.4 3.0 %copy-start.7 = (bf16[1,512,576]{1,2,0:T(8,128)(2,1)S(1)}, bf16[1,512,576]{1,2,0:T(8,128)(2,1)}, u32[]{:S(2)}) copy-start(bf16[1,512,576]{1,2,0:T(8,128)(2,1)} %param.26) | copy-start | bytes 1769476

commit v4 on v3

--- a/solution.py
+++ b/solution.py
@@ -125,10 +125,17 @@
     pd_size,
     pieces,
     window,
-    src,
+    select,
+    rows,
     weight,
+    drafts,
     out,
     weight_pair,
+    draft_slices,
+    src,
+    draft_own,
+    draft_send,
+    draft_recv,
     local_sem,
     weight_sem,
     pair_send,
@@ -166,13 +173,42 @@
             {"pd": lax.rem(column + step, pd_size)},
         )
 
+    def draft(mask):
+        return remote(
+            drafts.at[lax.div(me ^ mask, 2)],
+            draft_slices.at[lax.div(me, 2)],
+            draft_send.at[mask],
+            draft_recv.at[mask],
+            {"ep": me ^ mask},
+        )
+
+    def fill(mask):
+        src[me ^ mask] = jnp.dot(
+            select[me ^ mask], rows[...], preferred_element_type=jnp.float32
+        ).astype(jnp.bfloat16)
+
+    first = list(dict.fromkeys(mask for mask, _ in far[:window]))
+    for mask in first:
+        fill(mask)
     for item in far[:window]:
         direct(*item).start()
-    for item in near:
-        direct(*item).start()
+    fill(0)
     for piece in range(pieces):
         for step in range(1, pd_size):
             across(0, step, piece).start()
+    for item in near:
+        if item[1] == 0:
+            fill(item[0])
+        direct(*item).start()
+    for mask in list(dict.fromkeys(mask for mask, _ in far)):
+        if mask not in first:
+            fill(mask)
+    stay = pltpu.make_async_copy(
+        drafts.at[lax.div(me, 2)], draft_slices.at[lax.div(me, 2)], draft_own
+    )
+    stay.start()
+    for mask in range(2, ep_size, 2):
+        draft(mask).start()
     own = pltpu.make_async_copy(src.at[me], out.at[column, me], local_sem)
     own.start()
     core = lax.rem(me, 2)
@@ -193,6 +229,9 @@
     own.wait()
     keep.wait()
     give.wait()
+    stay.wait()
+    for mask in range(2, ep_size, 2):
+        draft(mask).wait()
     for item in near:
         direct(*item).wait_send()
     for mask in range(ep_size):
@@ -201,17 +240,24 @@
                 across(mask, step, piece).wait()
 
 
-def spread(source, weight, pieces, window, collective_id):
+def spread(select, rows, weight, drafts, pieces, window, collective_id):
     ep_size, pd_size = lax.axis_size("ep"), lax.axis_size("pd")
+    block_shape = select.shape[:2] + rows.shape[1:]
     return pl.pallas_call(
         functools.partial(spread_kernel, ep_size, pd_size, pieces, window),
         out_shape=(
-            jax.ShapeDtypeStruct((pd_size,) + source.shape, source.dtype),
+            jax.ShapeDtypeStruct((pd_size,) + block_shape, rows.dtype),
             jax.ShapeDtypeStruct((2,) + weight.shape, weight.dtype),
+            jax.ShapeDtypeStruct(drafts.shape, drafts.dtype),
         ),
-        in_specs=[pl.BlockSpec(memory_space=pl.ANY)] * 2,
-        out_specs=(pl.BlockSpec(memory_space=pl.ANY),) * 2,
+        in_specs=[pl.BlockSpec(memory_space=pltpu.VMEM)] * 2
+        + [pl.BlockSpec(memory_space=pl.ANY)] * 2,
+        out_specs=(pl.BlockSpec(memory_space=pl.ANY),) * 3,
         scratch_shapes=[
+            pltpu.VMEM(block_shape, rows.dtype),
+            pltpu.SemaphoreType.DMA,
+            pltpu.SemaphoreType.DMA((ep_size,)),
+            pltpu.SemaphoreType.DMA((ep_size,)),
             *([pltpu.SemaphoreType.DMA] * 4),
             pltpu.SemaphoreType.DMA((ep_size, pieces)),
             pltpu.SemaphoreType.DMA((ep_size, pieces)),
@@ -221,7 +267,7 @@
         compiler_params=pltpu.CompilerParams(
             collective_id=collective_id, has_side_effects=True, vmem_limit_bytes=40 * 2**20
         ),
-    )(source, weight)
+    )(select, rows, weight, drafts)
 
 
 def latent_kernel(
@@ -229,6 +275,7 @@
     pd_size,
     token_rows,
     slices,
+    draft_slices,
     weight,
     gain,
     out,
@@ -279,16 +326,19 @@
 
     for mask in far[:1] + near:
         outward(mask).start()
-    total = jnp.dot(slices[here], weight[...], preferred_element_type=jnp.float32)
+    def weighed(rows):
+        return jnp.dot(rows, weight[...], preferred_element_type=jnp.float32)
+
+    for mask in chips:
+        partial[chip(mask), token_rows:] = weighed(draft_slices[chip(mask)]).astype(jnp.bfloat16)
+    total = jnp.concatenate([weighed(slices[here]), weighed(draft_slices[here])], axis=0)
     for at, mask in enumerate(far):
         outward(mask).wait_send()
         for later in far[at + 1 : at + 2]:
             outward(later).start()
         for ready in [mask] if at else near + [mask]:
             outward(ready).wait_recv()
-            partial[chip(ready)] = jnp.dot(
-                arrived[chip(ready)], weight[...], preferred_element_type=jnp.float32
-            ).astype(jnp.bfloat16)
+            partial[chip(ready), :token_rows] = weighed(arrived[chip(ready)]).astype(jnp.bfloat16)
             homeward(ready).start()
     for mask in chips:
         homeward(mask).wait_recv()
@@ -357,9 +407,10 @@
             beside(mask, step).wait()
 
 
-def latents(slices, weight, gain, token_rows, collective_id):
+def latents(slices, draft_slices, weight, gain, collective_id):
     ep_size, pd_size = lax.axis_size("ep"), lax.axis_size("pd")
-    rows, width = slices.shape[1], weight.shape[1]
+    token_rows, width = slices.shape[1], weight.shape[1]
+    rows = token_rows + draft_slices.shape[1]
     vmem = pl.BlockSpec(memory_space=pltpu.VMEM)
     dma = pltpu.SemaphoreType.DMA
     return pl.pallas_call(
@@ -368,7 +419,7 @@
             jax.ShapeDtypeStruct((pd_size, ep_size, token_rows, width), jnp.bfloat16),
             jax.ShapeDtypeStruct((rows, width), jnp.bfloat16),
         ),
-        in_specs=[vmem] * 3,
+        in_specs=[vmem] * 4,
         out_specs=(vmem, vmem),
         scratch_shapes=[
             pltpu.VMEM(slices.shape, jnp.bfloat16),
@@ -381,7 +432,7 @@
         compiler_params=pltpu.CompilerParams(
             collective_id=collective_id, has_side_effects=True, vmem_limit_bytes=48 * 2**20
         ),
-    )(slices, weight, gain)
+    )(slices, draft_slices, weight, gain)
 
 
 def collect_kernel(
@@ -516,14 +567,18 @@
     )
     select = jnp.any(hits, axis=-1).astype(jnp.bfloat16)
     mix = jnp.sum(jnp.where(hits, route_weight[None], 0.0), axis=-1)
-    outgoing = (
-        jnp.dot(select, normed, preferred_element_type=jnp.float32)
-        .astype(jnp.bfloat16)
-        .reshape(experts, capacity, model_width)
-    )
+    slot_count, step_count = (draft_hidden.shape[0], draft_hidden.shape[1])
+    draft_rows = slot_count * step_count
+    draft_input = rms_norm(
+        draft_hidden.reshape(draft_rows, model_width).astype(jnp.float32), attn_gain
+    ).astype(jnp.bfloat16)
+    drafts = jnp.pad(draft_input, ((0, -draft_rows % 16), (0, 0)))
+    drafts = drafts.reshape(-1, experts // 2, 2 * kv_weight.shape[0]).swapaxes(0, 1)
     gate_local = gate_up[0]
     down_local = down_proj[0]
-    arrived, weight_pair = spread(outgoing, kv_weight, 4, 4, 1)
+    arrived, weight_pair, draft_slices = spread(
+        select.reshape(experts, capacity, tok_rows), normed, kv_weight, drafts, 4, 4, 1
+    )
     row_block = arrived.reshape(-1, model_width)
     gate_val = jnp.einsum("rd,dgf->rgf", row_block, gate_local, preferred_element_type=jnp.float32)
     partial_value = jnp.dot(
@@ -543,21 +598,12 @@
     )
     mixture = both[0] + both[1]
     layer_out = (hidden.astype(jnp.float32) + mixture).astype(jnp.bfloat16)
-    slot_count, step_count = (draft_hidden.shape[0], draft_hidden.shape[1])
     latent_width = kv_gain.shape[0]
     row_width = kv_weight.shape[1]
-    kv_input = rms_norm(
-        jnp.concatenate([layer_out, draft_hidden.reshape(-1, model_width)], axis=0).astype(
-            jnp.float32
-        ),
-        attn_gain,
-    ).astype(jnp.bfloat16)
-    spare = -kv_input.shape[0] % 16
-    slices = (
-        jnp.pad(kv_input, ((0, spare), (0, 0))).reshape(-1, experts // 2, 2 * kv_weight.shape[0])
-    ).swapaxes(0, 1)
+    kv_input = rms_norm(layer_out.astype(jnp.float32), attn_gain).astype(jnp.bfloat16)
+    slices = kv_input.reshape(tok_rows, experts // 2, 2 * kv_weight.shape[0]).swapaxes(0, 1)
     shard_rows, own_latent = latents(
-        slices, weight_pair.reshape(-1, row_width), kv_gain[None], tok_rows, 3
+        slices, draft_slices, weight_pair.reshape(-1, row_width), kv_gain[None], 3
     )
     draft_latent = own_latent[tok_rows : tok_rows + slot_count * step_count].reshape(
         slot_count, step_count, row_width

time: 287 us -> 281 us (0.979)
  matrix products: 28.6 us -> 24.4 us
    pallas_call x1, Pallas kernels: 89.3 us -> 105 us  [spread(): pl.pallas_call(functools.partial(spread_kernel, ep_size, pd_size, pieces,...]
    pallas_call x1, Pallas kernels: 97.7 us -> 88.2 us  [collect(): pl.pallas_call(functools.partial(collect_kernel, ep_size, pd_size, pieces...]
    pallas_call x1, Pallas kernels: 52.8 us -> 46.5 us  [latents(): pl.pallas_call(functools.partial(latent_kernel, ep_size, pd_size, token_r...]
    dot_general x1 -> x0, matrix products: 4.25 us -> none  [per_device(): jnp.dot(select, normed, preferred_element_type=jnp.float32)]
    unnamed x35 -> x39, local copies, waits for them, and re-layouts: 8.14 us -> 7.84 us
where the time goes in v4:
time: 281 us
  Pallas kernels  239 us (85%)
  matrix products  24.4 us (9%)
  local copies, waits for them, and re-layouts  9.29 us (3%)
  other arithmetic  5.63 us (2%)
    pallas_call x1, Pallas kernels, spread(): pl.pallas_call(functools.partial(spread_kernel, ep_size, pd_size, pieces,...  105 us
    pallas_call x1, Pallas kernels, collect(): pl.pallas_call(functools.partial(collect_kernel, ep_size, pd_size, pieces...  88.2 us
    pallas_call x1, Pallas kernels, latents(): pl.pallas_call(functools.partial(latent_kernel, ep_size, pd_size, token_r...  46.5 us
    dot_general x1, matrix products, per_device(): jnp.einsum('rd,dgf->rgf', row_block, gate_local, preferred_element_type=j...  11.3 us
    unnamed x39, local copies, waits for them, and re-layouts  7.84 us
    dot_general x1, matrix products, per_device(): jnp.dot((jax.nn.silu(gate_val[:, 0]) * gate_val[:, 1]).astype(jnp.bfloat1...  6.07 us

profile of v4, /device:TPU:0, one launch (start us, length us, event | category | flops | bytes accessed | tf_op | source)
XLA Modules:
  0.0 281.0 jit_solution(5815295679929761095)
XLA Ops:
  0.6 0.0 copy-start.5
  0.6 0.0 copy-start.12
  0.7 0.8 copy.54
  1.5 0.1 eq.126
  1.6 0.1 fusion.54
  1.7 0.2 reduce_window_sum.18
  1.9 0.2 select_reduce_fusion.1
  2.1 0.1 reduce_sum.86
  2.2 0.1 copy.55
  2.3 0.7 multiply_add_fusion
  3.0 0.1 fusion.43
  3.1 0.1 copy.56
  3.2 2.0 copy.58.weight
  5.3 0.0 copy-done.5
  5.3 0.0 copy-start.9
  5.3 0.0 copy-start.11
  5.3 0.3 fusion.6
  5.6 0.3 fusion.8.rows
  5.9 0.2 copy-done.9
  6.1 0.2 fusion.44
  6.3 0.1 fusion.46
  6.4 0.0 slice-start
  6.5 104.6 %shard_map.158 = (bf16[2,8,32,7168]{3,2,1,0:T(8,128)(2,1)S(1)}, bf16[2,896,576]{2,1,0:T(8,128)(2,1)S(1)}, bf16[4,16,1792]{2,1,0:T(8,128)(2,1)S(1)}) custom-call(bf16[8,32,64]{2,1,0:T(8,128)(2,1)S(1)} %bitcast.85, bf16[64,7168]{1,0:T(8,128)(2,1)S(1)} %fusion.8.rows, bf16[896,576]{1,0:T(8,128)(2,1)S(1)} %copy.58.weight, bf16[4,16,1792]{2,1,0:T(8,128)(2,1)S(1)} %bitcast.84), custom_call_target="tpu_custom_call" | custom-call | tf_op jit(solution)/shard_map/pallas_call | solution.py:246
  111.1 0.0 copy-start.1
  111.1 0.7 copy-done.1
  111.8 11.3 %fusion = f32[512,2,512]{2,0,1:T(8,128)S(1)} fusion(bf16[512,7168,1]{1,0,2:T(8,128)(2,1)S(1)} %bitcast.87, bf16[7168,2,512]{2,1,0:T(2,128)(2,1)} %bitcast.100), kind=kOutput, calls=%fused_computation | convolution fusion | flops 7516192768 | bytes 24117248 | tf_op jit(solution)/shard_map/rd,dgf->rgf/dot_general | solution.py:583
  123.1 6.1 %convolution_convert_fusion = bf16[512,7168]{1,0:T(8,128)(2,1)} fusion(bf16[1,512,7168]{2,1,0:T(8,128)(2,1)S(1)} %bitcast.102, f32[512,2,512]{2,0,1:T(8,128)S(1)} %fusion), kind=kOutput, calls=%fused_computation.2 | convolution fusion | flops 3763339264 | bytes 16777216 | tf_op jit(solution)/shard_map/dot_general | solution.py:584
  129.2 88.2 %shard_map.159 = bf16[8,32,7168]{2,1,0:T(8,128)(2,1)S(1)} custom-call(bf16[2,8,32,7168]{3,2,1,0:T(8,128)(2,1)} %bitcast.89), custom_call_target="tpu_custom_call" | custom-call | tf_op jit(solution)/shard_map/pallas_call | solution.py:513
  217.4 1.8 copy-done
  219.2 0.1 select_reduce_fusion
  219.4 0.0 copy-start.6
  219.4 2.8 fusion.49
  222.2 0.4 fusion.3
  222.6 0.0 copy-start.7
  222.6 0.0 copy-start.2
  222.6 0.0 copy-start.3
  222.6 0.3 fusion.5
  222.9 0.1 copy.74
  223.0 0.5 copy-done.7
  223.5 0.3 copy-done.2
  223.8 46.5 %shard_map.160 = (bf16[2,8,64,576]{3,2,1,0:T(8,128)(2,1)S(1)}, bf16[80,576]{1,0:T(8,128)(2,1)S(1)}) custom-call(bf16[4,64,1792]{2,1,0:T(8,128)(2,1)S(1)} %bitcast.82, bf16[4,16,1792]{2,1,0:T(8,128)(2,1)S(1)} %copy-done.2, bf16[1792,576]{1,0:T(8,128)(2,1)S(1)} %bitcast.83, f32[1,512]{1,0:T(1,128)S(1)} %bitcast.86), custom_call_target="tpu_custom_call" | custom-call | tf_op jit(solution)/shard_map/pallas_call | solution.py:416
  270.3 1.1 copy-done.4
  271.4 0.1 copy.61
  271.5 0.1 reduce.6
  271.6 0.7 fusion.87
  272.3 0.6 iota_compare_fusion.5
  273.0 0.7 iota_add_fusion
  273.6 0.0 copy-start.10
  273.6 2.0 convolution_convert_fusion.1
  276.4 0.3 fusion.17
  276.7 0.0 copy-start.8
  276.8 0.2 copy.64
  277.6 0.1 fusion.19
  277.8 0.1 multiply_cosine_fusion.1
  277.9 0.2 fusion.15
  278.1 0.1 pad_add_fusion
  278.2 0.1 broadcast_in_dim.78
  278.3 0.4 copy.65
  278.7 0.3 copy.60
  279.0 0.5 fusion.96
  279.5 0.2 fusion.37
  279.6 0.1 divide_convert_fusion
  279.8 0.2 copy.66
  279.9 1.1 fusion.12
  (42 shorter events, 0.4 us)
Async XLA Ops:
  0.6 4.6 %copy-start.5 = (bf16[64,7168]{1,0:T(8,128)(2,1)S(1)}, bf16[64,7168]{1,0:T(8,128)(2,1)}, u32[]{:S(2)}) copy-start(bf16[64,7168]{1,0:T(8,128)(2,1)} %param.15) | copy-start | bytes 2752516
  0.6 4.9 %copy-start.12 = (f32[7168]{0:T(1024)S(1)}, f32[7168]{0:T(1024)}, u32[]{:S(2)}) copy-start(f32[7168]{0:T(1024)} %param.16) | copy-start | bytes 86020
  5.3 0.8 copy-start.9
  5.3 1.0 copy-start.11
  6.4 116.6 %slice-start = ((s8[7340032]{0:T(1024)(128)(4,1)}), s8[4194304]{0:T(1024)(128)(4,1)S(1)}, s32[]{:S(2)}) async-start(s8[7340032]{0:T(1024)(128)(4,1)} %bitcast.101), calls=%async_computation | async-start | bytes 8388608
  111.1 0.7 copy-start.1
  111.8 11.3 %slice-start.1 = ((s8[7340032]{0:T(1024)(128)(4,1)}), s8[3145728]{0:T(1024)(128)(4,1)S(1)}, s32[]{:S(2)}) async-start(s8[7340032]{0:T(1024)(128)(4,1)} %bitcast.101), calls=%async_computation.1 | async-start | bytes 6291456
  129.2 90.0 %copy-start.13 = (f32[64,2]{0,1:T(2,128)S(1)}, f32[64,2]{0,1:T(2,128)}, u32[]{:S(2)}) copy-start(f32[64,2]{0,1:T(2,128)} %param.18) | copy-start | bytes 1540
  217.4 1.8 copy-start
  219.4 2.8 copy-start.6
  222.6 0.9 copy-start.7
  222.6 1.2 copy-start.2
  222.6 1.2 copy-start.3
  223.5 47.9 %copy-start.14 = (s32[16]{0:T(128)S(1)}, s32[16]{0:T(128)}, u32[]{:S(2)}) copy-start(s32[16]{0:T(128)} %param.24) | copy-start | bytes 196
  223.5 48.1 %copy-start.15 = (s32[16]{0:T(128)S(1)}, s32[16]{0:T(128)}, u32[]{:S(2)}) copy-start(s32[16]{0:T(128)} %param.25) | copy-start | bytes 196
  270.3 1.1 copy-start.4
  273.6 4.3 %copy-start.10 = (bf16[1,4,64,576]{3,2,1,0:T(8,128)(2,1)S(1)}, bf16[1,4,64,576]{3,2,1,0:T(8,128)(2,1)}, u32[]{:S(2)}) copy-start(bf16[1,4,64,576]{3,2,1,0:T(8,128)(2,1)} %param.29) | copy-start | bytes 884740
  276.7 1.9 copy-start.8
